TPU v7x, 256 devices: a whole 4x4x8 slice. The times are simulated.
256 devices in a mesh: pair: 32 (over z, y_hi, core), band: 8 (over y_lo, x).
Axes of the slice: x: 4, y: 4 (y_hi: 2, y_lo: 2; y = y_hi * 2 + y_lo), z: 8, core: 2. Of those that a mesh axis runs over, the one named last changes fastest.
Arguments:
- spectra: bfloat16 [2, 512, 4096, 256], P(None, 'band', 'pair'), may hold values from -600 to 600, as said below
- live: int32 [4096], P('pair'), may hold values 0 or 1
Outputs:
- correlations: float32 [524288, 256], P(('pair', 'band'))
Inputs may be any that keep to these rules, and one draw needn't show every extreme that they name: `spectra`: finite values.
All inputs are finite; a program needn't handle non-finite values. No bound on the sum of `live` on one device may be relied on, other than what follows from the above.
Results may differ from a plain program's by a relative error of at most 0.017.
Values may be sent and summed in bfloat16 or wider, within the bound.
No kernel may reach another device: no remote copies, remote signals or barrier semaphores. Data moves between devices by JAX's collectives and lax.ppermute only.
A program may use at most 128 MiB of HBM per device.

v0:
```python
import jax
import jax.numpy as jnp
from jax import lax
from jax.sharding import PartitionSpec as P

LAGS = 256
NFFT = 2048
K0 = 64
OFFSET = 5


def from_behind(value, axis, steps):
    count = lax.axis_size(axis)
    pairs = [(source, (source + steps) % count) for source in range(count)]
    return lax.ppermute(value, axis, pairs)


def lag_tables(first, count, lags):
    freq = first + jnp.arange(count, dtype=jnp.int32)
    lag_index = jnp.arange(lags, dtype=jnp.int32) - lags // 2
    phase = freq[:, None] * lag_index[None, :] % NFFT
    angle = phase.astype(jnp.float32) * (2.0 * jnp.pi / NFFT)
    return jnp.stack([jnp.cos(angle), -jnp.sin(angle)]).astype(jnp.bfloat16)


def local(spectra, live):
    freq_local = spectra.shape[1]
    channels = spectra.shape[2]
    windows = spectra.shape[3]
    bands = lax.axis_size("band")
    masked = spectra.astype(jnp.float32) * live.astype(jnp.float32)[None, None, :, None]
    amplitude = jnp.sqrt(jnp.mean(masked[0] * masked[0] + masked[1] * masked[1], axis=2) + 1e-06)
    white = (masked / amplitude[None, :, :, None]).astype(jnp.bfloat16)
    partner = from_behind(white, "pair", -OFFSET)
    product = jnp.einsum("sfaw,tfbw->stfab", white, partner, preferred_element_type=jnp.float32)
    inv_windows = 1.0 / jnp.sqrt(jnp.float32(windows))
    real_part = (product[0, 0] + product[1, 1]) * inv_windows
    imag_part = (product[1, 0] - product[0, 1]) * inv_windows
    cross = (
        jnp.stack([real_part, imag_part])
        .reshape(2, freq_local, channels * channels)
        .astype(jnp.bfloat16)
    )
    all_freq = freq_local * bands
    inv_freq = 1.0 / jnp.sqrt(jnp.float32(all_freq))
    first = K0 + lax.axis_index("band") * freq_local
    local_table = lag_tables(first, freq_local, LAGS)
    summed = jnp.einsum("sfp,sfl->pl", cross, local_table, preferred_element_type=jnp.float32)
    return lax.psum_scatter(
        (summed * inv_freq).astype(jnp.bfloat16), "band", scatter_dimension=0, tiled=True
    ).astype(jnp.float32)


def solution(mesh):
    in_specs = (P(None, "band", "pair", None), P("pair"))
    out_specs = P(("pair", "band"), None)
    return jax.shard_map(local, mesh=mesh, in_specs=in_specs, out_specs=out_specs, check_vma=False)
```

profile of v0, /device:TPU:1, one launch (start us, length us, event | category | flops | bytes accessed | tf_op | source)
XLA Modules:
  0.0 457.3 jit_solution(16162764078014001300)
XLA Ops:
  6.5 0.0 reduce-scatter.2.cloned.1.call-start
  6.5 0.7 convert_element_type.32
  7.2 11.6 %convert_multiply_fusion = f32[2,64,128,256]{3,2,0,1:T(8,128)} fusion(bf16[2,64,128,256]{3,2,1,0:T(8,128)(2,1)} %param.2, f32[128]{0:T(128)S(1)} %convert_element_type.32), kind=kLoop, calls=%fused_computation.4 | loop fusion | flops 8388608 | bytes 25166336 | tf_op jit(solution)/shard_map/mul | solution.py:31
  18.8 0.0 copy-start
  18.8 6.6 %fusion.3 = f32[64,128]{1,0:T(8,128)S(1)} fusion(f32[2,64,128,256]{3,2,0,1:T(8,128)} %convert_multiply_fusion), kind=kLoop, calls=%fused_computation.8 | loop fusion | flops 8380416 | bytes 16809984 | tf_op jit(solution)/shard_map/reduce_sum | solution.py:32
  25.5 1.6 copy-done
  27.1 4.6 %divide_convert_fusion = bf16[2,64,128,256]{3,2,0,1:T(8,128)(2,1)} fusion(f32[64,128]{1,0:T(8,128)S(1)} %add_sqrt_fusion, f32[128]{0:T(128)S(1)} %convert_element_type.32, bf16[2,64,128,256]{3,2,1,0:T(8,128)(2,1)S(1)} %copy-done), kind=kLoop, calls=%fused_computation.3 | loop fusion | flops 16777216 | bytes 16810496 | tf_op jit(solution)/shard_map/convert_element_type | solution.py:33
  31.6 7.0 %collective-permute-start = (bf16[2,64,128,256]{3,2,0,1:T(8,128)(2,1)}, bf16[2,64,128,256]{3,2,0,1:T(8,128)(2,1)}, u32[]{:S(2)}, u32[]{:S(2)}) collective-permute-start(bf16[2,64,128,256]{3,2,0,1:T(8,128)(2,1)} %divide_convert_fusion), channel_id=1, source_target_pairs={{0,216},{8,224},{16,232},{24,240},{32,248},{40,0},{48,8},{56,16},{... | collective-permute-start | bytes 25165832 | tf_op jit(solution)/shard_map/ppermute | solution.py:15
  38.6 0.3 cosine_convert_fusion
  39.0 266.4 %collective-permute-done = bf16[2,64,128,256]{3,2,0,1:T(8,128)(2,1)} collective-permute-done((bf16[2,64,128,256]{3,2,0,1:T(8,128)(2,1)}, bf16[2,64,128,256]{3,2,0,1:T(8,128)(2,1)}, u32[]{:S(2)}, u32[]{:S(2)}) %collective-permute-start) | collective-permute-done | bytes 8388640 | tf_op jit(solution)/shard_map/ppermute | solution.py:15
  305.4 13.9 %convolution_bitcast_fusion.1 = f32[2,2,64,128,128]{3,4,0,1,2:T(8,128)} fusion(bf16[2,64,128,256]{3,2,0,1:T(8,128)(2,1)} %divide_convert_fusion, bf16[2,64,128,256]{3,2,0,1:T(8,128)(2,1)} %collective-permute-done), kind=kOutput, calls=%fused_computation.5 | convolution fusion | flops 2147483648 | bytes 33554432 | tf_op jit(solution)/shard_map/sfaw,tfbw->stfab/dot_general | solution.py:35
  319.3 8.2 %fusion.9 = (bf16[1,1,64,128,128]{3,4,0,1,2:T(8,128)(2,1)S(1)}, bf16[1,1,64,128,128]{3,4,0,1,2:T(8,128)(2,1)}) fusion(f32[2,2,64,128,128]{3,4,0,1,2:T(8,128)} %convolution_bitcast_fusion.1), kind=kLoop, calls=%fused_computation.17 | loop fusion | flops 6291456 | bytes 20971520 | tf_op jit(solution)/shard_map/convert.5
  327.4 4.1 copy.6
  331.5 4.2 mul.101
  335.7 2.9 copy.5
  338.6 2.8 mul.99
  341.4 7.2 %fusion.1 = bf16[16384,256]{1,0:T(8,128)(2,1)} fusion(bf16[1,64,16384]{2,1,0:T(8,128)(2,1)} %mul.101, bf16[1,64,16384]{2,1,0:T(8,128)(2,1)S(1)} %mul.99, bf16[1,64,256]{2,1,0:T(8,128)(2,1)S(1)} %get-tuple-element.8, bf16[1,64,256]{2,1,0:T(8,128)(2,1)S(1)} %get-tuple-element.7), kind=kOutput, calls=%fused_computation.2 | convolution fusion | flops 1084260352 | bytes 12648448 | tf_op jit(solution)/shard_map/sfp,sfl->pl/dot_general | solution.py:48
  348.6 0.0 reduce-scatter.2.cloned.1.call-update
  348.6 99.1 %reduce-scatter.2.cloned.1.call-done = bf16[2048,256]{1,0:T(8,128)(2,1)} async-done(((bf16[16384,256]{1,0:T(8,128)(2,1)}), bf16[2048,256]{1,0:T(8,128)(2,1)}) %reduce-scatter.2.cloned.1.call-update) | async-done | bytes 1048592 | tf_op jit(solution)/shard_map/reduce_scatter | solution.py:49
  447.7 2.7 convert_element_type.36
  (3 shorter events, 0.0 us)
Async XLA Ops:
  6.5 441.2 %reduce-scatter.2.cloned.1.call-start = ((), (), s32[]{:S(2)}) async-start(), calls=%async_computation.1 | async-start | bytes 9437184 | tf_op jit(solution)/shard_map/reduce_scatter | solution.py:49
  18.8 8.2 %copy-start = (bf16[2,64,128,256]{3,2,1,0:T(8,128)(2,1)S(1)}, bf16[2,64,128,256]{3,2,1,0:T(8,128)(2,1)}, u32[]{:S(2)}) copy-start(bf16[2,64,128,256]{3,2,1,0:T(8,128)(2,1)} %param.2) | copy-start | bytes 25165828
  31.6 273.8 %collective-permute-start = (bf16[2,64,128,256]{3,2,0,1:T(8,128)(2,1)}, bf16[2,64,128,256]{3,2,0,1:T(8,128)(2,1)}, u32[]{:S(2)}, u32[]{:S(2)}) collective-permute-start(bf16[2,64,128,256]{3,2,0,1:T(8,128)(2,1)} %divide_convert_fusion), channel_id=1, source_target_pairs={{0,216},{8,224},{16,232},{24,240},{32,248},{40,0},{48,8},{56,16},{... | collective-permute-start | bytes 25165832 | tf_op jit(solution)/shard_map/ppermute | solution.py:15
Sparse Core Ops, SparseCore 0:
  348.7 98.9 reduce-scatter.1
where the time goes:
time: 458 us; the launch traced here: 457 us
  waiting for transfers between devices  366 us (80%)
  other arithmetic  34.7 us (8%)
  matrix products  21.1 us (5%)
  local copies, waits for them, and re-layouts  15.5 us (3%)
  between operations  13.4 us (3%)
  starting transfers between devices  6.97 us (2%)
    ppermute x1, waiting for transfers between devices, from_behind(): return lax.ppermute(value, axis, pairs)  266 us
    reduce_scatter x1, waiting for transfers between devices, local(): lax.psum_scatter((summed * inv_freq).astype(jnp.bfloat16), 'band', scatte...  99.1 us
    dot_general x1, matrix products, local(): jnp.einsum('sfaw,tfbw->stfab', white, partner, preferred_element_type=jnp...  13.9 us
    mul x1, other arithmetic, local(): spectra.astype(jnp.float32) * live.astype(jnp.float32)[None, None, :, None]  11.6 us
  transfers between devices with their start and end apart: 2, of which 2 were waited for; matrix products, arithmetic and copies ran while one was open for 0% of the time, Pallas kernels for 0%

commit v1 on v0

v1 whole, which is shorter than its diff:
```python
import functools

import jax
import jax.numpy as jnp
from jax import lax
from jax.experimental import pallas as pl
from jax.experimental.pallas import tpu as pltpu
from jax.sharding import PartitionSpec as P

LAGS = 256
NFFT = 2048
K0 = 64
OFFSET = 5
CHUNK = 8
STEP = 2


def shift(value, axis, steps):
    count = lax.axis_size(axis)
    pairs = [(source, (source + steps) % count) for source in range(count)]
    return lax.ppermute(value, axis, pairs)


def whiten_kernel(x_ref, live_ref, o_ref):
    live = live_ref[...]
    windows = x_ref.shape[3]
    for f in range(x_ref.shape[1]):
        real = x_ref[0, f].astype(jnp.float32)
        imag = x_ref[1, f].astype(jnp.float32)
        power = jnp.sum(real * real + imag * imag, axis=1, keepdims=True) * (1.0 / windows)
        scale = live * lax.rsqrt(live * live * power + 1e-06)
        o_ref[f, 0] = (real * scale).astype(jnp.bfloat16)
        o_ref[f, 1] = (imag * scale).astype(jnp.bfloat16)


def whiten(spectra, live, chunk):
    _, _, channels, windows = spectra.shape
    steps = CHUNK // STEP
    return pl.pallas_call(
        whiten_kernel,
        grid=(steps,),
        in_specs=[
            pl.BlockSpec((2, STEP, channels, windows), lambda i: (0, chunk * steps + i, 0, 0)),
            pl.BlockSpec((channels, 1), lambda i: (0, 0)),
        ],
        out_specs=pl.BlockSpec((STEP, 2, channels, windows), lambda i: (i, 0, 0, 0)),
        out_shape=jax.ShapeDtypeStruct((CHUNK, 2, channels, windows), jnp.bfloat16),
        cost_estimate=pl.CostEstimate(
            flops=8 * 2 * CHUNK * channels * windows,
            bytes_accessed=8 * CHUNK * channels * windows,
            transcendentals=0,
        ),
        name="whiten",
    )(spectra, live)


def cross_kernel(x_ref, y_ref, o_ref, acc):
    count, _, channels, windows = x_ref.shape
    depth = 2 * count
    norm = 1.0 / windows**0.5
    for f in range(count):
        x = x_ref[f].reshape(2 * channels, windows)
        y = y_ref[f].reshape(2 * channels, windows)
        product = lax.dot_general(
            x, y, (((1,), (1,)), ((), ())), preferred_element_type=jnp.float32
        )
        low, high = product[:channels], product[channels:]
        real = low[:, :channels] + high[:, channels:]
        imag = high[:, :channels] - low[:, channels:]
        acc[pl.ds(f, channels, stride=depth), :] = real * norm
        acc[pl.ds(count + f, channels, stride=depth), :] = imag * norm
    o_ref[...] = acc[...].astype(jnp.bfloat16)


def cross(x, y):
    count, _, channels, windows = x.shape
    rows = channels * 2 * count
    return pl.pallas_call(
        cross_kernel,
        out_shape=jax.ShapeDtypeStruct((rows, channels), jnp.bfloat16),
        scratch_shapes=[pltpu.VMEM((rows, channels), jnp.float32)],
        cost_estimate=pl.CostEstimate(
            flops=8 * count * channels * channels * windows,
            bytes_accessed=8 * count * channels * windows + 2 * rows * channels,
            transcendentals=0,
        ),
        compiler_params=pltpu.CompilerParams(vmem_limit_bytes=32 * 1024 * 1024),
        name="cross",
    )(x, y)


def lags_kernel(parts, norm, *refs):
    piece_refs, table_ref, o_ref = refs[:parts], refs[parts], refs[parts + 1]
    bands, rows, channels = piece_refs[0].shape
    depth = 2 * CHUNK
    for a in range(rows // depth):
        columns = jnp.concatenate(
            [ref[band, a * depth : (a + 1) * depth, :] for ref in piece_refs for band in range(bands)],
            axis=0,
        )
        total = lax.dot_general(
            columns, table_ref[...], (((0,), (0,)), ((), ())), preferred_element_type=jnp.float32
        )
        o_ref[a * channels : (a + 1) * channels, :] = (total * norm).astype(o_ref.dtype)


def to_lags(pieces, table, norm, dtype):
    bands, rows, channels = pieces[0].shape
    pairs = rows // (2 * CHUNK) * channels
    lags = table.shape[1]
    return pl.pallas_call(
        functools.partial(lags_kernel, len(pieces), norm),
        out_shape=jax.ShapeDtypeStruct((pairs, lags), dtype),
        cost_estimate=pl.CostEstimate(
            flops=2 * pairs * lags * table.shape[0],
            bytes_accessed=2 * pairs * table.shape[0] + 4 * pairs * lags,
            transcendentals=0,
        ),
        compiler_params=pltpu.CompilerParams(vmem_limit_bytes=32 * 1024 * 1024),
        name="to_lags",
    )(*pieces, table)


def lag_table(chunks, bands, freq_local):
    chunk = jnp.asarray(chunks, jnp.int32)[:, None, None]
    band = jnp.arange(bands, dtype=jnp.int32)[None, :, None]
    inner = jnp.arange(CHUNK, dtype=jnp.int32)[None, None, :]
    freq = K0 + band * freq_local + chunk * CHUNK + inner
    lag_index = jnp.arange(LAGS, dtype=jnp.int32) - LAGS // 2
    phase = freq[..., None] * lag_index % NFFT
    angle = phase.astype(jnp.float32) * (2.0 * jnp.pi / NFFT)
    table = jnp.stack([jnp.cos(angle), -jnp.sin(angle)], axis=2)
    return table.reshape(-1, LAGS).astype(jnp.bfloat16)


def local(spectra, live):
    _, freq_local, channels, windows = spectra.shape
    bands = lax.axis_size("band")
    chunks = freq_local // CHUNK
    up = list(range(chunks // 2))
    down = list(range(chunks // 2, chunks))
    norm = 1.0 / float(freq_local * bands) ** 0.5
    mask = live.astype(jnp.float32)[:, None]
    white = [whiten(spectra, mask, chunk) for chunk in range(chunks)]

    def exchange(own, other):
        value = cross(own, other).reshape(bands, -1, channels)
        return lax.all_to_all(value, "band", 0, 0)

    up_pieces, down_pieces = [], []
    up_got, down_got = [], []
    for u, d in zip(up, down):
        send_up, send_down = white[u], white[d]
        if len(up_got) >= 2:
            send_up, _ = lax.optimization_barrier((send_up, up_got[-2]))
            send_down, _ = lax.optimization_barrier((send_down, down_got[-2]))
        up_got.append(shift(send_up, "pair", OFFSET))
        down_got.append(shift(send_down, "pair", -OFFSET))
    for step, (u, d) in enumerate(zip(up, down)):
        up_pieces.append(exchange(up_got[step], white[u]))
        down_pieces.append(exchange(white[d], down_got[step]))
    back = to_lags(up_pieces, lag_table(up, bands, freq_local), norm, jnp.bfloat16)
    back = shift(back, "pair", -OFFSET)
    here = to_lags(down_pieces, lag_table(down, bands, freq_local), norm, jnp.float32)
    return here + back.astype(jnp.float32)


def solution(mesh):
    in_specs = (P(None, "band", "pair", None), P("pair"))
    out_specs = P(("pair", "band"), None)
    return jax.shard_map(local, mesh=mesh, in_specs=in_specs, out_specs=out_specs, check_vma=False)
```

time: 458 us -> 246 us (0.54)
  waiting for transfers between devices: 366 us -> 67.2 us
  starting transfers between devices: 6.97 us -> 115 us
  Pallas kernels: 0 us -> 55.2 us
  other arithmetic: 34.7 us -> 5.91 us
  matrix products: 21.1 us -> 0 us
  local copies, waits for them, and re-layouts: 15.5 us -> 0.79 us
  between operations: 13.4 us -> 0.11 us
    ppermute x1 -> x9, waiting for transfers between devices: 266 us -> 52.7 us  [shift(): return lax.ppermute(value, axis, pairs)]
    reduce_scatter x1 -> x0, waiting for transfers between devices: 99.1 us -> none  [local(): lax.psum_scatter((summed * inv_freq).astype(jnp.bfloat16), 'band', scatte...]
    ppermute x1 -> x9, starting transfers between devices: 6.97 us -> 68.8 us  [shift(): return lax.ppermute(value, axis, pairs)]
    pallas_call x0 -> x18, Pallas kernels: none -> 55.2 us  [the longest x8 31 us: whiten(): pl.pallas_call(whiten_kernel, grid=(steps,), in_specs=[pl.BlockSpec((2, S...]
    all_to_all x0 -> x8, starting transfers between devices: none -> 46.3 us  [exchange(): return lax.all_to_all(value, 'band', 0, 0)]
    dot_general x2 -> x0, matrix products: 21.1 us -> none  [the longest x1 13.9 us: local(): jnp.einsum('sfaw,tfbw->stfab', white, partner, preferred_element_type=jnp...]
    all_to_all x0 -> x8, waiting for transfers between devices: none -> 14.5 us  [exchange(): return lax.all_to_all(value, 'band', 0, 0)]
    mul x1, other arithmetic: 11.6 us -> 0.01 us  [lag_table(): freq = K0 + band * freq_local + chunk * CHUNK + inner]
  transfers between devices with their start and end apart: 2 -> 17, of which waited for: 2 -> 6; matrix products, arithmetic and copies ran while one was open for 0% -> 1% of each run, Pallas kernels for 0% -> 21%
where the time goes in v1:
time: 246 us; the launch traced here: 244 us
  starting transfers between devices  115 us (47%)
  waiting for transfers between devices  67.2 us (27%)
  Pallas kernels  55.2 us (22%)
  other arithmetic  5.91 us (2%)
    ppermute x9, starting transfers between devices, shift(): return lax.ppermute(value, axis, pairs)  68.8 us
    ppermute x9, waiting for transfers between devices, shift(): return lax.ppermute(value, axis, pairs)  52.7 us
    all_to_all x8, starting transfers between devices, exchange(): return lax.all_to_all(value, 'band', 0, 0)  46.3 us
    pallas_call x8, Pallas kernels, whiten(): pl.pallas_call(whiten_kernel, grid=(steps,), in_specs=[pl.BlockSpec((2, S...  31 us
    pallas_call x8, Pallas kernels, cross(): pl.pallas_call(cross_kernel, out_shape=jax.ShapeDtypeStruct((rows, channe...  20.5 us
    all_to_all x8, waiting for transfers between devices, exchange(): return lax.all_to_all(value, 'band', 0, 0)  14.5 us
  transfers between devices with their start and end apart: 17, of which 6 were waited for; matrix products, arithmetic and copies ran while one was open for 1% of the time, Pallas kernels for 21%

profile of v1, /device:TPU:1, one launch (start us, length us, event | category | flops | bytes accessed | tf_op | source)
XLA Modules:
  0.0 244.3 jit_solution(10572355198847719427)
XLA Ops:
  0.0 0.7 convert_bitcast_fusion
  0.7 0.7 copy.5.live_ref
  1.4 3.8 %whiten.8.x_ref = bf16[8,2,128,256]{3,2,1,0:T(8,128)(2,1)} custom-call(bf16[2,64,128,256]{3,2,1,0:T(8,128)(2,1)} %x_ref.15, f32[128,1]{1,0:T(8,128)} %copy.5.live_ref), custom_call_target="tpu_custom_call" | custom-call | flops 4194304 | bytes 2097152 | tf_op jit(solution)/shard_map/whiten/pallas_call | solution.py:39
  5.2 7.0 %collective-permute-start = (bf16[8,2,128,256]{3,2,1,0:T(8,128)(2,1)}, bf16[8,2,128,256]{3,2,1,0:T(8,128)(2,1)}, u32[]{:S(2)}, u32[]{:S(2)}) collective-permute-start(bf16[8,2,128,256]{3,2,1,0:T(8,128)(2,1)} %whiten.8.x_ref), channel_id=1, source_target_pairs={{0,216},{8,224},{16,232},{24,240},{32,248},{40,0},{48,8},{56,16},{... | collective-permute-start | bytes 3145736 | tf_op jit(solution)/shard_map/ppermute | solution.py:21
  12.2 3.8 %whiten.12.y_ref = bf16[8,2,128,256]{3,2,1,0:T(8,128)(2,1)} custom-call(bf16[2,64,128,256]{3,2,1,0:T(8,128)(2,1)} %x_ref.15, f32[128,1]{1,0:T(8,128)} %copy.5.live_ref), custom_call_target="tpu_custom_call" | custom-call | flops 4194304 | bytes 2097152 | tf_op jit(solution)/shard_map/whiten/pallas_call | solution.py:39
  16.0 3.9 %whiten.13.y_ref = bf16[8,2,128,256]{3,2,1,0:T(8,128)(2,1)} custom-call(bf16[2,64,128,256]{3,2,1,0:T(8,128)(2,1)} %x_ref.15, f32[128,1]{1,0:T(8,128)} %copy.5.live_ref), custom_call_target="tpu_custom_call" | custom-call | flops 4194304 | bytes 2097152 | tf_op jit(solution)/shard_map/whiten/pallas_call | solution.py:39
  19.9 0.3 collective-permute-start.5
  20.2 22.8 %collective-permute-done.y_ref = bf16[8,2,128,256]{3,2,1,0:T(8,128)(2,1)} collective-permute-done((bf16[8,2,128,256]{3,2,1,0:T(8,128)(2,1)}, bf16[8,2,128,256]{3,2,1,0:T(8,128)(2,1)}, u32[]{:S(2)}, u32[]{:S(2)}) %collective-permute-start) | collective-permute-done | bytes 1048608 | tf_op jit(solution)/shard_map/ppermute | solution.py:21
  43.0 2.7 %cross.8 = bf16[2048,128]{1,0:T(8,128)(2,1)} custom-call(bf16[8,2,128,256]{3,2,1,0:T(8,128)(2,1)S(1)} %copy-done.7, bf16[8,2,128,256]{3,2,1,0:T(8,128)(2,1)} %collective-permute-done.y_ref), custom_call_target="tpu_custom_call" | custom-call | flops 268435456 | bytes 2621440 | tf_op jit(solution)/shard_map/cross/pallas_call | solution.py:78
  45.7 6.5 %all-to-all-start = ((bf16[8,256,128]{2,1,0:T(8,128)(2,1)}), bf16[8,256,128]{2,1,0:T(8,128)(2,1)S(1)}, u32[]{:S(2)}, u32[]{:S(2)}) async-start(bf16[8,256,128]{2,1,0:T(8,128)(2,1)} %bitcast.1), calls=%async_computation | async-start | bytes 1048576 | tf_op jit(solution)/shard_map/all_to_all | solution.py:148
  52.2 3.9 %whiten.14.y_ref = bf16[8,2,128,256]{3,2,1,0:T(8,128)(2,1)} custom-call(bf16[2,64,128,256]{3,2,1,0:T(8,128)(2,1)} %x_ref.15, f32[128,1]{1,0:T(8,128)} %copy.5.live_ref), custom_call_target="tpu_custom_call" | custom-call | flops 4194304 | bytes 2097152 | tf_op jit(solution)/shard_map/whiten/pallas_call | solution.py:39
  56.1 0.0 collective-permute-done.4.x_ref
  56.1 0.0 collective-permute-start.6
  56.1 1.5 cross.12
  57.6 2.8 %all-to-all-done.refs_0_ = bf16[8,256,128]{2,1,0:T(8,128)(2,1)S(1)} async-done(((bf16[8,256,128]{2,1,0:T(8,128)(2,1)}), bf16[8,256,128]{2,1,0:T(8,128)(2,1)S(1)}, u32[]{:S(2)}, u32[]{:S(2)}) %all-to-all-start) | async-done | bytes 524320 | tf_op jit(solution)/shard_map/all_to_all | solution.py:148
  60.4 9.8 %all-to-all-start.4 = ((bf16[8,256,128]{2,1,0:T(8,128)(2,1)}), bf16[8,256,128]{2,1,0:T(8,128)(2,1)S(1)}, u32[]{:S(2)}, u32[]{:S(2)}) async-start(bf16[8,256,128]{2,1,0:T(8,128)(2,1)} %bitcast.6), calls=%async_computation.4 | async-start | bytes 1048576 | tf_op jit(solution)/shard_map/all_to_all | solution.py:148
  70.2 3.9 %whiten.15.y_ref = bf16[8,2,128,256]{3,2,1,0:T(8,128)(2,1)} custom-call(bf16[2,64,128,256]{3,2,1,0:T(8,128)(2,1)} %x_ref.15, f32[128,1]{1,0:T(8,128)} %copy.5.live_ref), custom_call_target="tpu_custom_call" | custom-call | flops 4194304 | bytes 2097152 | tf_op jit(solution)/shard_map/whiten/pallas_call | solution.py:39
  74.1 0.0 collective-permute-done.5.x_ref
  74.1 6.8 %collective-permute-start.7 = (bf16[8,2,128,256]{3,2,1,0:T(8,128)(2,1)}, bf16[8,2,128,256]{3,2,1,0:T(8,128)(2,1)}, u32[]{:S(2)}, u32[]{:S(2)}) collective-permute-start(bf16[8,2,128,256]{3,2,1,0:T(8,128)(2,1)} %whiten.15.y_ref), channel_id=1, source_target_pairs={{0,40},{8,48},{16,56},{24,64},{32,72},{40,80},{48,88},{56,96},{64,... | collective-permute-start | bytes 3145736 | tf_op jit(solution)/shard_map/ppermute | solution.py:21
  80.9 2.7 %cross.13 = bf16[2048,128]{1,0:T(8,128)(2,1)} custom-call(bf16[8,2,128,256]{3,2,1,0:T(8,128)(2,1)} %collective-permute-done.5.x_ref, bf16[8,2,128,256]{3,2,1,0:T(8,128)(2,1)S(1)} %copy-done.5), custom_call_target="tpu_custom_call" | custom-call | flops 268435456 | bytes 2621440 | tf_op jit(solution)/shard_map/cross/pallas_call | solution.py:78
  83.6 4.8 %all-to-all-start.5 = ((bf16[8,256,128]{2,1,0:T(8,128)(2,1)}), bf16[8,256,128]{2,1,0:T(8,128)(2,1)S(1)}, u32[]{:S(2)}, u32[]{:S(2)}) async-start(bf16[8,256,128]{2,1,0:T(8,128)(2,1)} %bitcast.7), calls=%async_computation.5 | async-start | bytes 1048576 | tf_op jit(solution)/shard_map/all_to_all | solution.py:148
  88.4 3.9 %whiten.9.x_ref = bf16[8,2,128,256]{3,2,1,0:T(8,128)(2,1)} custom-call(bf16[2,64,128,256]{3,2,1,0:T(8,128)(2,1)} %x_ref.15, f32[128,1]{1,0:T(8,128)} %copy.5.live_ref), custom_call_target="tpu_custom_call" | custom-call | flops 4194304 | bytes 2097152 | tf_op jit(solution)/shard_map/whiten/pallas_call | solution.py:39
  92.3 12.4 %collective-permute-start.1 = (bf16[8,2,128,256]{3,2,1,0:T(8,128)(2,1)}, bf16[8,2,128,256]{3,2,1,0:T(8,128)(2,1)}, u32[]{:S(2)}, u32[]{:S(2)}) collective-permute-start(bf16[8,2,128,256]{3,2,1,0:T(8,128)(2,1)} %whiten.9.x_ref), channel_id=1, source_target_pairs={{0,216},{8,224},{16,232},{24,240},{32,248},{40,0},{48,8},{56,16},{... | collective-permute-start | bytes 3145736 | tf_op jit(solution)/shard_map/ppermute | solution.py:21
  104.7 2.7 %cross.14 = bf16[2048,128]{1,0:T(8,128)(2,1)} custom-call(bf16[8,2,128,256]{3,2,1,0:T(8,128)(2,1)} %collective-permute-done.6.x_ref, bf16[8,2,128,256]{3,2,1,0:T(8,128)(2,1)S(1)} %copy-done.4), custom_call_target="tpu_custom_call" | custom-call | flops 268435456 | bytes 2621440 | tf_op jit(solution)/shard_map/cross/pallas_call | solution.py:78
  107.4 5.4 %all-to-all-start.6 = ((bf16[8,256,128]{2,1,0:T(8,128)(2,1)}), bf16[8,256,128]{2,1,0:T(8,128)(2,1)S(1)}, u32[]{:S(2)}, u32[]{:S(2)}) async-start(bf16[8,256,128]{2,1,0:T(8,128)(2,1)} %bitcast.8), calls=%async_computation.6 | async-start | bytes 1048576 | tf_op jit(solution)/shard_map/all_to_all | solution.py:148
  112.8 3.9 %whiten.10.x_ref = bf16[8,2,128,256]{3,2,1,0:T(8,128)(2,1)} custom-call(bf16[2,64,128,256]{3,2,1,0:T(8,128)(2,1)} %x_ref.15, f32[128,1]{1,0:T(8,128)} %copy.5.live_ref), custom_call_target="tpu_custom_call" | custom-call | flops 4194304 | bytes 2097152 | tf_op jit(solution)/shard_map/whiten/pallas_call | solution.py:39
  116.7 22.0 %collective-permute-start.2 = (bf16[8,2,128,256]{3,2,1,0:T(8,128)(2,1)}, bf16[8,2,128,256]{3,2,1,0:T(8,128)(2,1)}, u32[]{:S(2)}, u32[]{:S(2)}) collective-permute-start(bf16[8,2,128,256]{3,2,1,0:T(8,128)(2,1)} %whiten.10.x_ref), channel_id=1, source_target_pairs={{0,216},{8,224},{16,232},{24,240},{32,248},{40,0},{48,8},{56,16},{... | collective-permute-start | bytes 3145736 | tf_op jit(solution)/shard_map/ppermute | solution.py:21
  138.8 2.7 %cross.15 = bf16[2048,128]{1,0:T(8,128)(2,1)} custom-call(bf16[8,2,128,256]{3,2,1,0:T(8,128)(2,1)} %collective-permute-done.7.x_ref, bf16[8,2,128,256]{3,2,1,0:T(8,128)(2,1)S(1)} %copy-done.3), custom_call_target="tpu_custom_call" | custom-call | flops 268435456 | bytes 2621440 | tf_op jit(solution)/shard_map/cross/pallas_call | solution.py:78
  141.5 5.4 %all-to-all-start.7 = ((bf16[8,256,128]{2,1,0:T(8,128)(2,1)}), bf16[8,256,128]{2,1,0:T(8,128)(2,1)}, u32[]{:S(2)}, u32[]{:S(2)}) async-start(bf16[8,256,128]{2,1,0:T(8,128)(2,1)} %bitcast.9), calls=%async_computation.7 | async-start | bytes 1048576 | tf_op jit(solution)/shard_map/all_to_all | solution.py:148
  146.9 0.1 broadcast_add_fusion
  147.0 3.9 %whiten.11.x_ref = bf16[8,2,128,256]{3,2,1,0:T(8,128)(2,1)} custom-call(bf16[2,64,128,256]{3,2,1,0:T(8,128)(2,1)} %x_ref.15, f32[128,1]{1,0:T(8,128)} %copy.5.live_ref), custom_call_target="tpu_custom_call" | custom-call | flops 4194304 | bytes 2097152 | tf_op jit(solution)/shard_map/whiten/pallas_call | solution.py:39
  150.9 0.1 iota_add_fusion
  151.0 19.8 %collective-permute-start.3 = (bf16[8,2,128,256]{3,2,1,0:T(8,128)(2,1)}, bf16[8,2,128,256]{3,2,1,0:T(8,128)(2,1)}, u32[]{:S(2)}, u32[]{:S(2)}) collective-permute-start(bf16[8,2,128,256]{3,2,1,0:T(8,128)(2,1)} %whiten.11.x_ref), channel_id=1, source_target_pairs={{0,216},{8,224},{16,232},{24,240},{32,248},{40,0},{48,8},{56,16},{... | collective-permute-start | bytes 3145736 | tf_op jit(solution)/shard_map/ppermute | solution.py:21
  170.8 2.7 %cross.9 = bf16[2048,128]{1,0:T(8,128)(2,1)} custom-call(bf16[8,2,128,256]{3,2,1,0:T(8,128)(2,1)S(1)} %copy-done.2, bf16[8,2,128,256]{3,2,1,0:T(8,128)(2,1)} %collective-permute-done.1.y_ref), custom_call_target="tpu_custom_call" | custom-call | flops 268435456 | bytes 2621440 | tf_op jit(solution)/shard_map/cross/pallas_call | solution.py:78
  173.5 5.6 %all-to-all-start.1 = ((bf16[8,256,128]{2,1,0:T(8,128)(2,1)}), bf16[8,256,128]{2,1,0:T(8,128)(2,1)S(1)}, u32[]{:S(2)}, u32[]{:S(2)}) async-start(bf16[8,256,128]{2,1,0:T(8,128)(2,1)} %bitcast.2), calls=%async_computation.1 | async-start | bytes 1048576 | tf_op jit(solution)/shard_map/all_to_all | solution.py:148
  179.1 2.3 cosine_convert_fusion
  181.4 2.9 %to_lags.3 = bf16[2048,256]{1,0:T(8,128)(2,1)} custom-call(bf16[8,256,128]{2,1,0:T(8,128)(2,1)S(1)} %all-to-all-done.4.refs_0_, bf16[8,256,128]{2,1,0:T(8,128)(2,1)S(1)} %all-to-all-done.5.refs_1_, bf16[8,256,128]{2,1,0:T(8,128)(2,1)S(1)} %copy-done.9, bf16[8,256,128]{2,1,0:T(8,128)(2,1)} %all-to-all-done.7.refs_3_, bf16[512,256]{1,0:T(8,128)(2,1)S(1)} %bitcast.13), custom_call_target="tpu_custom_call" | custom-call | flops 536870912 | bytes 4194304 | tf_op jit(solution)/shard_map/to_lags/pallas_call | solution.py:111
  184.3 0.6 collective-permute-start.8
  184.8 2.7 %cross.10 = bf16[2048,128]{1,0:T(8,128)(2,1)} custom-call(bf16[8,2,128,256]{3,2,1,0:T(8,128)(2,1)S(1)} %copy-done, bf16[8,2,128,256]{3,2,1,0:T(8,128)(2,1)} %collective-permute-done.2.y_ref), custom_call_target="tpu_custom_call" | custom-call | flops 268435456 | bytes 2621440 | tf_op jit(solution)/shard_map/cross/pallas_call | solution.py:78
  187.6 1.9 all-to-all-done.1.refs_1_
  189.4 3.6 %all-to-all-start.2 = ((bf16[8,256,128]{2,1,0:T(8,128)(2,1)}), bf16[8,256,128]{2,1,0:T(8,128)(2,1)S(1)}, u32[]{:S(2)}, u32[]{:S(2)}) async-start(bf16[8,256,128]{2,1,0:T(8,128)(2,1)} %bitcast.3), calls=%async_computation.2 | async-start | bytes 1048576 | tf_op jit(solution)/shard_map/all_to_all | solution.py:148
  193.0 14.1 %collective-permute-done.3.y_ref = bf16[8,2,128,256]{3,2,1,0:T(8,128)(2,1)} collective-permute-done((bf16[8,2,128,256]{3,2,1,0:T(8,128)(2,1)}, bf16[8,2,128,256]{3,2,1,0:T(8,128)(2,1)}, u32[]{:S(2)}, u32[]{:S(2)}) %collective-permute-start.3) | collective-permute-done | bytes 1048608 | tf_op jit(solution)/shard_map/ppermute | solution.py:21
  207.1 2.7 %cross.11 = bf16[2048,128]{1,0:T(8,128)(2,1)} custom-call(bf16[8,2,128,256]{3,2,1,0:T(8,128)(2,1)S(1)} %copy-done.1, bf16[8,2,128,256]{3,2,1,0:T(8,128)(2,1)} %collective-permute-done.3.y_ref), custom_call_target="tpu_custom_call" | custom-call | flops 268435456 | bytes 2621440 | tf_op jit(solution)/shard_map/cross/pallas_call | solution.py:78
  209.8 5.3 %all-to-all-start.3 = ((bf16[8,256,128]{2,1,0:T(8,128)(2,1)}), bf16[8,256,128]{2,1,0:T(8,128)(2,1)S(1)}, u32[]{:S(2)}, u32[]{:S(2)}) async-start(bf16[8,256,128]{2,1,0:T(8,128)(2,1)} %bitcast.4), calls=%async_computation.3 | async-start | bytes 1048576 | tf_op jit(solution)/shard_map/all_to_all | solution.py:148
  215.2 9.8 %all-to-all-done.3.refs_3_ = bf16[8,256,128]{2,1,0:T(8,128)(2,1)S(1)} async-done(((bf16[8,256,128]{2,1,0:T(8,128)(2,1)}), bf16[8,256,128]{2,1,0:T(8,128)(2,1)S(1)}, u32[]{:S(2)}, u32[]{:S(2)}) %all-to-all-start.3) | async-done | bytes 524320 | tf_op jit(solution)/shard_map/all_to_all | solution.py:148
  225.0 0.8 to_lags.2
  225.8 15.8 %collective-permute-done.8 = bf16[2048,256]{1,0:T(8,128)(2,1)} collective-permute-done((bf16[2048,256]{1,0:T(8,128)(2,1)}, bf16[2048,256]{1,0:T(8,128)(2,1)}, u32[]{:S(2)}, u32[]{:S(2)}) %collective-permute-start.8) | collective-permute-done | bytes 1048608 | tf_op jit(solution)/shard_map/ppermute | solution.py:21
  241.6 2.7 %convert_add_fusion = f32[2048,256]{1,0:T(8,128)} fusion(f32[2048,256]{1,0:T(8,128)S(1)} %to_lags.2, bf16[2048,256]{1,0:T(8,128)(2,1)} %collective-permute-done.8), kind=kLoop, calls=%fused_computation | loop fusion | flops 1048576 | bytes 5242880 | tf_op jit(solution)/shard_map/add | solution.py:165
  (37 shorter events, 0.1 us)
Async XLA Ops:
  5.2 37.8 %collective-permute-start = (bf16[8,2,128,256]{3,2,1,0:T(8,128)(2,1)}, bf16[8,2,128,256]{3,2,1,0:T(8,128)(2,1)}, u32[]{:S(2)}, u32[]{:S(2)}) collective-permute-start(bf16[8,2,128,256]{3,2,1,0:T(8,128)(2,1)} %whiten.8.x_ref), channel_id=1, source_target_pairs={{0,216},{8,224},{16,232},{24,240},{32,248},{40,0},{48,8},{56,16},{... | collective-permute-start | bytes 3145736 | tf_op jit(solution)/shard_map/ppermute | solution.py:21
  16.0 27.0 %copy-start.7 = (bf16[8,2,128,256]{3,2,1,0:T(8,128)(2,1)S(1)}, bf16[8,2,128,256]{3,2,1,0:T(8,128)(2,1)}, u32[]{:S(2)}) copy-start(bf16[8,2,128,256]{3,2,1,0:T(8,128)(2,1)} %whiten.8.x_ref) | copy-start | bytes 3145732
  16.0 40.1 %collective-permute-start.4 = (bf16[8,2,128,256]{3,2,1,0:T(8,128)(2,1)}, bf16[8,2,128,256]{3,2,1,0:T(8,128)(2,1)S(1)}, u32[]{:S(2)}, u32[]{:S(2)}) collective-permute-start(bf16[8,2,128,256]{3,2,1,0:T(8,128)(2,1)} %whiten.12.y_ref), channel_id=1, source_target_pairs={{0,40},{8,48},{16,56},{24,64},{32,72},{40,80},{48,88},{56,96},{64,... | collective-permute-start | bytes 3145736 | tf_op jit(solution)/shard_map/ppermute | solution.py:21
  19.9 54.2 %collective-permute-start.5 = (bf16[8,2,128,256]{3,2,1,0:T(8,128)(2,1)}, bf16[8,2,128,256]{3,2,1,0:T(8,128)(2,1)}, u32[]{:S(2)}, u32[]{:S(2)}) collective-permute-start(bf16[8,2,128,256]{3,2,1,0:T(8,128)(2,1)} %whiten.13.y_ref), channel_id=1, source_target_pairs={{0,40},{8,48},{16,56},{24,64},{32,72},{40,80},{48,88},{56,96},{64,... | collective-permute-start | bytes 3145736 | tf_op jit(solution)/shard_map/ppermute | solution.py:21
  45.7 14.6 %all-to-all-start = ((bf16[8,256,128]{2,1,0:T(8,128)(2,1)}), bf16[8,256,128]{2,1,0:T(8,128)(2,1)S(1)}, u32[]{:S(2)}, u32[]{:S(2)}) async-start(bf16[8,256,128]{2,1,0:T(8,128)(2,1)} %bitcast.1), calls=%async_computation | async-start | bytes 1048576 | tf_op jit(solution)/shard_map/all_to_all | solution.py:148
  52.2 3.9 %copy-start.6 = (bf16[8,2,128,256]{3,2,1,0:T(8,128)(2,1)S(1)}, bf16[8,2,128,256]{3,2,1,0:T(8,128)(2,1)}, u32[]{:S(2)}) copy-start(bf16[8,2,128,256]{3,2,1,0:T(8,128)(2,1)} %whiten.12.y_ref) | copy-start | bytes 3145732
  56.1 48.6 %collective-permute-start.6 = (bf16[8,2,128,256]{3,2,1,0:T(8,128)(2,1)}, bf16[8,2,128,256]{3,2,1,0:T(8,128)(2,1)}, u32[]{:S(2)}, u32[]{:S(2)}) collective-permute-start(bf16[8,2,128,256]{3,2,1,0:T(8,128)(2,1)} %whiten.14.y_ref), channel_id=1, source_target_pairs={{0,40},{8,48},{16,56},{24,64},{32,72},{40,80},{48,88},{56,96},{64,... | collective-permute-start | bytes 3145736 | tf_op jit(solution)/shard_map/ppermute | solution.py:21
  60.4 23.3 %all-to-all-start.4 = ((bf16[8,256,128]{2,1,0:T(8,128)(2,1)}), bf16[8,256,128]{2,1,0:T(8,128)(2,1)S(1)}, u32[]{:S(2)}, u32[]{:S(2)}) async-start(bf16[8,256,128]{2,1,0:T(8,128)(2,1)} %bitcast.6), calls=%async_computation.4 | async-start | bytes 1048576 | tf_op jit(solution)/shard_map/all_to_all | solution.py:148
  70.2 10.7 %copy-start.5 = (bf16[8,2,128,256]{3,2,1,0:T(8,128)(2,1)S(1)}, bf16[8,2,128,256]{3,2,1,0:T(8,128)(2,1)}, u32[]{:S(2)}) copy-start(bf16[8,2,128,256]{3,2,1,0:T(8,128)(2,1)} %whiten.13.y_ref) | copy-start | bytes 3145732
  74.1 64.6 %collective-permute-start.7 = (bf16[8,2,128,256]{3,2,1,0:T(8,128)(2,1)}, bf16[8,2,128,256]{3,2,1,0:T(8,128)(2,1)}, u32[]{:S(2)}, u32[]{:S(2)}) collective-permute-start(bf16[8,2,128,256]{3,2,1,0:T(8,128)(2,1)} %whiten.15.y_ref), channel_id=1, source_target_pairs={{0,40},{8,48},{16,56},{24,64},{32,72},{40,80},{48,88},{56,96},{64,... | collective-permute-start | bytes 3145736 | tf_op jit(solution)/shard_map/ppermute | solution.py:21
  83.6 23.8 %all-to-all-start.5 = ((bf16[8,256,128]{2,1,0:T(8,128)(2,1)}), bf16[8,256,128]{2,1,0:T(8,128)(2,1)S(1)}, u32[]{:S(2)}, u32[]{:S(2)}) async-start(bf16[8,256,128]{2,1,0:T(8,128)(2,1)} %bitcast.7), calls=%async_computation.5 | async-start | bytes 1048576 | tf_op jit(solution)/shard_map/all_to_all | solution.py:148
  88.4 16.3 %copy-start.4 = (bf16[8,2,128,256]{3,2,1,0:T(8,128)(2,1)S(1)}, bf16[8,2,128,256]{3,2,1,0:T(8,128)(2,1)}, u32[]{:S(2)}) copy-start(bf16[8,2,128,256]{3,2,1,0:T(8,128)(2,1)} %whiten.14.y_ref) | copy-start | bytes 3145732
  92.3 58.7 %collective-permute-start.1 = (bf16[8,2,128,256]{3,2,1,0:T(8,128)(2,1)}, bf16[8,2,128,256]{3,2,1,0:T(8,128)(2,1)}, u32[]{:S(2)}, u32[]{:S(2)}) collective-permute-start(bf16[8,2,128,256]{3,2,1,0:T(8,128)(2,1)} %whiten.9.x_ref), channel_id=1, source_target_pairs={{0,216},{8,224},{16,232},{24,240},{32,248},{40,0},{48,8},{56,16},{... | collective-permute-start | bytes 3145736 | tf_op jit(solution)/shard_map/ppermute | solution.py:21
  107.4 34.1 %all-to-all-start.6 = ((bf16[8,256,128]{2,1,0:T(8,128)(2,1)}), bf16[8,256,128]{2,1,0:T(8,128)(2,1)S(1)}, u32[]{:S(2)}, u32[]{:S(2)}) async-start(bf16[8,256,128]{2,1,0:T(8,128)(2,1)} %bitcast.8), calls=%async_computation.6 | async-start | bytes 1048576 | tf_op jit(solution)/shard_map/all_to_all | solution.py:148
  112.8 25.9 %copy-start.3 = (bf16[8,2,128,256]{3,2,1,0:T(8,128)(2,1)S(1)}, bf16[8,2,128,256]{3,2,1,0:T(8,128)(2,1)}, u32[]{:S(2)}) copy-start(bf16[8,2,128,256]{3,2,1,0:T(8,128)(2,1)} %whiten.15.y_ref) | copy-start | bytes 3145732
  116.7 30.2 %copy-start.10 = (s32[4]{0:T(128)S(1)}, s32[4]{0:T(128)}, u32[]{:S(2)}) copy-start(s32[4]{0:T(128)} %constant.34) | copy-start | bytes 52
  116.7 68.1 %collective-permute-start.2 = (bf16[8,2,128,256]{3,2,1,0:T(8,128)(2,1)}, bf16[8,2,128,256]{3,2,1,0:T(8,128)(2,1)}, u32[]{:S(2)}, u32[]{:S(2)}) collective-permute-start(bf16[8,2,128,256]{3,2,1,0:T(8,128)(2,1)} %whiten.10.x_ref), channel_id=1, source_target_pairs={{0,216},{8,224},{16,232},{24,240},{32,248},{40,0},{48,8},{56,16},{... | collective-permute-start | bytes 3145736 | tf_op jit(solution)/shard_map/ppermute | solution.py:21
  141.5 9.4 %copy-start.8 = (bf16[8,256,128]{2,1,0:T(8,128)(2,1)}, bf16[8,256,128]{2,1,0:T(8,128)(2,1)S(1)}, u32[]{:S(2)}) copy-start(bf16[8,256,128]{2,1,0:T(8,128)(2,1)S(1)} %all-to-all-done.6.refs_2_) | copy-start | bytes 1572868
  141.5 32.0 %all-to-all-start.7 = ((bf16[8,256,128]{2,1,0:T(8,128)(2,1)}), bf16[8,256,128]{2,1,0:T(8,128)(2,1)}, u32[]{:S(2)}, u32[]{:S(2)}) async-start(bf16[8,256,128]{2,1,0:T(8,128)(2,1)} %bitcast.9), calls=%async_computation.7 | async-start | bytes 1048576 | tf_op jit(solution)/shard_map/all_to_all | solution.py:148
  147.0 23.8 %copy-start.2 = (bf16[8,2,128,256]{3,2,1,0:T(8,128)(2,1)S(1)}, bf16[8,2,128,256]{3,2,1,0:T(8,128)(2,1)}, u32[]{:S(2)}) copy-start(bf16[8,2,128,256]{3,2,1,0:T(8,128)(2,1)} %whiten.9.x_ref) | copy-start | bytes 3145732
  151.0 56.2 %collective-permute-start.3 = (bf16[8,2,128,256]{3,2,1,0:T(8,128)(2,1)}, bf16[8,2,128,256]{3,2,1,0:T(8,128)(2,1)}, u32[]{:S(2)}, u32[]{:S(2)}) collective-permute-start(bf16[8,2,128,256]{3,2,1,0:T(8,128)(2,1)} %whiten.11.x_ref), channel_id=1, source_target_pairs={{0,216},{8,224},{16,232},{24,240},{32,248},{40,0},{48,8},{56,16},{... | collective-permute-start | bytes 3145736 | tf_op jit(solution)/shard_map/ppermute | solution.py:21
  173.5 7.9 %copy-start.9 = (bf16[8,256,128]{2,1,0:T(8,128)(2,1)S(1)}, bf16[8,256,128]{2,1,0:T(8,128)(2,1)}, u32[]{:S(2)}) copy-start(bf16[8,256,128]{2,1,0:T(8,128)(2,1)} %copy-done.8) | copy-start | bytes 1572868
  173.5 15.9 %all-to-all-start.1 = ((bf16[8,256,128]{2,1,0:T(8,128)(2,1)}), bf16[8,256,128]{2,1,0:T(8,128)(2,1)S(1)}, u32[]{:S(2)}, u32[]{:S(2)}) async-start(bf16[8,256,128]{2,1,0:T(8,128)(2,1)} %bitcast.2), calls=%async_computation.1 | async-start | bytes 1048576 | tf_op jit(solution)/shard_map/all_to_all | solution.py:148
  181.4 3.5 %copy-start = (bf16[8,2,128,256]{3,2,1,0:T(8,128)(2,1)S(1)}, bf16[8,2,128,256]{3,2,1,0:T(8,128)(2,1)}, u32[]{:S(2)}) copy-start(bf16[8,2,128,256]{3,2,1,0:T(8,128)(2,1)} %whiten.10.x_ref) | copy-start | bytes 3145732
  184.3 22.8 %copy-start.1 = (bf16[8,2,128,256]{3,2,1,0:T(8,128)(2,1)S(1)}, bf16[8,2,128,256]{3,2,1,0:T(8,128)(2,1)}, u32[]{:S(2)}) copy-start(bf16[8,2,128,256]{3,2,1,0:T(8,128)(2,1)} %whiten.11.x_ref) | copy-start | bytes 3145732
  184.3 57.3 %collective-permute-start.8 = (bf16[2048,256]{1,0:T(8,128)(2,1)}, bf16[2048,256]{1,0:T(8,128)(2,1)}, u32[]{:S(2)}, u32[]{:S(2)}) collective-permute-start(bf16[2048,256]{1,0:T(8,128)(2,1)} %to_lags.3), channel_id=1, source_target_pairs={{0,216},{8,224},{16,232},{24,240},{32,248},{40,0},{48,8},{56,16},{... | collective-permute-start | bytes 3145736 | tf_op jit(solution)/shard_map/ppermute | solution.py:21
  189.4 20.4 %all-to-all-start.2 = ((bf16[8,256,128]{2,1,0:T(8,128)(2,1)}), bf16[8,256,128]{2,1,0:T(8,128)(2,1)S(1)}, u32[]{:S(2)}, u32[]{:S(2)}) async-start(bf16[8,256,128]{2,1,0:T(8,128)(2,1)} %bitcast.3), calls=%async_computation.2 | async-start | bytes 1048576 | tf_op jit(solution)/shard_map/all_to_all | solution.py:148
  209.8 15.2 %all-to-all-start.3 = ((bf16[8,256,128]{2,1,0:T(8,128)(2,1)}), bf16[8,256,128]{2,1,0:T(8,128)(2,1)S(1)}, u32[]{:S(2)}, u32[]{:S(2)}) async-start(bf16[8,256,128]{2,1,0:T(8,128)(2,1)} %bitcast.4), calls=%async_computation.3 | async-start | bytes 1048576 | tf_op jit(solution)/shard_map/all_to_all | solution.py:148

commit v2 on v0

v2 whole, which is shorter than its diff:
```python
import functools

import jax
import jax.numpy as jnp
from jax import lax
from jax.experimental import pallas as pl
from jax.experimental.pallas import tpu as pltpu
from jax.sharding import PartitionSpec as P

LAGS = 256
NFFT = 2048
K0 = 64
OFFSET = 5
STEP = 4
GROUPS = (("down", 1), ("up", 1), ("up", 1), ("down", 1), ("up", 1), ("up", 1), ("down", 1), ("up", 1))
WHITEN = (2, 6)
PLAN = (
    ("send", 0),
    ("send", 1),
    ("send", 2),
    ("send", 3),
    ("send", 4),
    ("join", (0, 1), "t", "s"),
    ("send", 5, "v0"),
    ("join", (2, 4), "v0", "g3"),
    ("send", 7, "p0"),
    ("send", 6, "g5"),
    ("join", (5,), "v1", "p0"),
    ("join", (7,), "v2", "p1"),
    ("join", (3, 6), "v3", "p2"),
)


def whiten_kernel(starts, x_ref, live_ref, *o_refs):
    live = live_ref[...]
    windows = x_ref.shape[3]
    step = pl.program_id(0)

    def write(o_ref):
        for f in range(STEP):
            real = x_ref[0, f].astype(jnp.float32)
            imag = x_ref[1, f].astype(jnp.float32)
            power = jnp.sum(real * real + imag * imag, axis=1, keepdims=True) * (1.0 / windows)
            scale = live * lax.rsqrt(live * live * power + 1e-06)
            o_ref[f, 0] = (real * scale).astype(jnp.bfloat16)
            o_ref[f, 1] = (imag * scale).astype(jnp.bfloat16)

    for k, o_ref in enumerate(o_refs):
        pl.when((step >= starts[k]) & (step < starts[k + 1]))(functools.partial(write, o_ref))


def whiten(spectra, live, first, counts):
    _, _, channels, windows = spectra.shape
    steps = [count // STEP for count in counts]
    starts = [sum(steps[:k]) for k in range(len(steps) + 1)]

    def out_block(k):
        return lambda i: (jnp.clip(i - starts[k], 0, steps[k] - 1), 0, 0, 0)

    return pl.pallas_call(
        functools.partial(whiten_kernel, starts),
        grid=(starts[-1],),
        in_specs=[
            pl.BlockSpec((2, STEP, channels, windows), lambda i: (0, first // STEP + i, 0, 0)),
            pl.BlockSpec((channels, 1), lambda i: (0, 0)),
        ],
        out_specs=[
            pl.BlockSpec((STEP, 2, channels, windows), out_block(k)) for k in range(len(counts))
        ],
        out_shape=[
            jax.ShapeDtypeStruct((count, 2, channels, windows), jnp.bfloat16) for count in counts
        ],
        cost_estimate=pl.CostEstimate(
            flops=16 * sum(counts) * channels * windows,
            bytes_accessed=8 * sum(counts) * channels * windows,
            transcendentals=0,
        ),
        name="whiten",
    )(spectra, live)


def cross_kernel(shapes, pick_ref, *refs):
    *refs, o_ref, acc = refs
    bands = o_ref.shape[0]
    place = 0
    for sources in shapes:
        x_ref, y_refs, refs = refs[0], refs[1 : 1 + sources], refs[1 + sources :]
        count, _, channels, windows = x_ref.shape
        depth = 2 * count
        norm = 1.0 / windows**0.5
        for f in range(count):
            x = x_ref[f].reshape(2 * channels, windows)
            y = y_refs[0][f]
            if sources > 1:
                y = jnp.where(pick_ref[0] > 0, y_refs[1][f], y)
            y = y.reshape(2 * channels, windows)
            product = lax.dot_general(
                x, y, (((1,), (1,)), ((), ())), preferred_element_type=jnp.float32
            )
            low, high = product[:channels], product[channels:]
            real = low[:, :channels] + high[:, channels:]
            imag = high[:, :channels] - low[:, channels:]
            acc[pl.ds(f, channels, stride=depth), :] = real * norm
            acc[pl.ds(count + f, channels, stride=depth), :] = imag * norm
        rows = channels * depth // bands
        for band in range(bands):
            part = acc[band * rows : (band + 1) * rows, :]
            o_ref[band, place : place + rows, :] = part.astype(jnp.bfloat16)
        place += rows


def cross(groups, pick, bands):
    channels = groups[0][0].shape[2]
    rows = [channels * 2 * x.shape[0] for x, _ in groups]
    work = sum(x.size for x, _ in groups)
    return pl.pallas_call(
        functools.partial(cross_kernel, [len(ys) for _, ys in groups]),
        in_specs=[pl.BlockSpec(memory_space=pltpu.SMEM)]
        + [pl.BlockSpec(memory_space=pltpu.VMEM)] * sum(1 + len(ys) for _, ys in groups),
        out_shape=jax.ShapeDtypeStruct((bands, sum(rows) // bands, channels), jnp.bfloat16),
        scratch_shapes=[pltpu.VMEM((max(rows), channels), jnp.float32)],
        compiler_params=pltpu.CompilerParams(vmem_limit_bytes=40 * 1024 * 1024),
        cost_estimate=pl.CostEstimate(
            flops=4 * work * channels, bytes_accessed=5 * work, transcendentals=0
        ),
        name="cross",
    )(pick, *[ref for x, ys in groups for ref in (x, *ys)])


def lags_kernel(norm, places, *refs):
    *piece_refs, table_ref, o_ref = refs
    rows, channels = o_ref.shape[0], piece_refs[0].shape[2]
    for a in range(rows // channels):
        columns = []
        for ref, (place, depth) in zip(piece_refs, places):
            start = place + a * depth
            columns += [ref[band, start : start + depth, :] for band in range(ref.shape[0])]
        total = lax.dot_general(
            jnp.concatenate(columns, axis=0),
            table_ref[...],
            (((0,), (0,)), ((), ())),
            preferred_element_type=jnp.float32,
        )
        o_ref[a * channels : (a + 1) * channels, :] = (total * norm).astype(o_ref.dtype)


def to_lags(pieces, table, norm, dtype):
    bands, _, channels = pieces[0][0].shape
    pairs = channels * channels // bands
    lags = table.shape[1]
    return pl.pallas_call(
        functools.partial(lags_kernel, norm, [(place, depth) for _, place, depth in pieces]),
        out_shape=jax.ShapeDtypeStruct((pairs, lags), dtype),
        compiler_params=pltpu.CompilerParams(vmem_limit_bytes=32 * 1024 * 1024),
        cost_estimate=pl.CostEstimate(
            flops=2 * pairs * table.size,
            bytes_accessed=2 * pairs * table.shape[0] + 4 * pairs * lags,
            transcendentals=0,
        ),
        name="to_lags",
    )(*[piece for piece, _, _ in pieces], table)


def lag_table(first, count, bands, freq_local):
    band = jnp.arange(bands, dtype=jnp.int32)[:, None]
    freq = K0 + band * freq_local + first + jnp.arange(count, dtype=jnp.int32)
    lag_index = jnp.arange(LAGS, dtype=jnp.int32) - LAGS // 2
    phase = freq[..., None] * lag_index % NFFT
    angle = phase.astype(jnp.float32) * (2.0 * jnp.pi / NFFT)
    table = jnp.stack([jnp.cos(angle), -jnp.sin(angle)], axis=1)
    return table.reshape(-1, LAGS).astype(jnp.bfloat16)


def routes(blocks):
    behind, ahead, third, back = [], [], [], []
    for i in range(blocks):
        partner = (i + OFFSET) % blocks
        place = (partner, partner - 2, i + 1, partner + 2)[i % 4] % blocks
        behind.append((partner, i))
        ahead.append((i, place))
        back.append((place, i))
        if place != partner:
            third.append((partner, place))
    return behind, ahead, third, back


def local(spectra, live):
    _, freq_local, channels, windows = spectra.shape
    bands = lax.axis_size("band")
    behind, ahead, third, back = routes(lax.axis_size("pair"))
    norm = 1.0 / float(freq_local * bands) ** 0.5
    mask = live.astype(jnp.float32)[:, None]
    pick = (lax.axis_index("pair") % 4 != 1).astype(jnp.int32)[None]
    counts = [eighths * freq_local // 8 for _, eighths in GROUPS]
    firsts = [sum(counts[:k]) for k in range(len(counts))]

    def after(own, earlier):
        return lax.optimization_barrier((own, earlier))[0]

    white = []
    for members in WHITEN:
        source = after(spectra, white[-1]) if white else spectra
        white += whiten(source, mask, firsts[len(white)], counts[len(white) : len(white) + members])

    table = {
        way: jnp.concatenate(
            [
                lag_table(firsts[k], counts[k], bands, freq_local)
                for kind, what, *_ in PLAN
                if kind == "join"
                for k in what
                if GROUPS[k][0] == way
            ]
        )
        for way in ("up", "down")
    }
    there = {"t": table["up"], "s": table["down"]}
    arrived = {}
    pieces = {"up": [], "down": []}
    for kind, what, *needs in PLAN:
        if kind == "send":
            way, own = GROUPS[what][0], white[what]
            sent = own
            for need in needs:
                sent = after(sent, there[need])
            moved = lax.ppermute(sent, "pair", ahead if way == "up" else behind)
            there[f"g{what}"] = moved
            if way == "up":
                arrived[what] = (moved, [own, lax.ppermute(sent, "pair", third)])
            else:
                arrived[what] = (own, [moved])
            continue
        factors = [arrived[k] for k in what]
        for need in needs:
            factors[0] = (after(factors[0][0], there[need]), factors[0][1])
        value = cross(factors, pick, bands)
        piece = lax.all_to_all(value, "band", 0, 0)
        number = sum(name[0] == "v" for name in there)
        there[f"v{number}"], there[f"p{number}"] = value, piece
        place = 0
        for k in what:
            way = GROUPS[k][0]
            pieces[way].append((piece, place, 2 * counts[k]))
            place += channels // bands * 2 * counts[k]
    far = to_lags(pieces["up"], table["up"], norm, jnp.bfloat16)
    far = lax.ppermute(far, "pair", back)
    near = to_lags(pieces["down"], table["down"], norm, jnp.float32)
    return near + far.astype(jnp.float32)


def solution(mesh):
    in_specs = (P(None, "band", "pair", None), P("pair"))
    out_specs = P(("pair", "band"), None)
    return jax.shard_map(local, mesh=mesh, in_specs=in_specs, out_specs=out_specs, check_vma=False)
```

time: 458 us -> 196 us (0.43)
  the two profiles are of different devices: /device:TPU:1 before, /device:TPU:97 now
where the time goes in v2:
time: 196 us; the launch traced here: 195 us
  starting transfers between devices  95.6 us (49%)
  Pallas kernels  34.5 us (18%)
  waiting for transfers between devices  29.6 us (15%)
  blocking collectives  26.4 us (13%)
  other arithmetic  5.06 us (3%)
  local copies, waits for them, and re-layouts  3.72 us (2%)
    ppermute x8, starting transfers between devices, local(): moved = lax.ppermute(sent, 'pair', ahead if way == 'up' else behind)  46.8 us
    all_to_all x3, starting transfers between devices, local(): piece = lax.all_to_all(value, 'band', 0, 0)  29.9 us
    all_to_all x2, blocking collectives, local(): piece = lax.all_to_all(value, 'band', 0, 0)  26.4 us
    pallas_call x5, Pallas kernels, cross(): pl.pallas_call(functools.partial(cross_kernel, [len(ys) for _, ys in grou...  16.8 us
    pallas_call x2, Pallas kernels, whiten(): pl.pallas_call(functools.partial(whiten_kernel, starts), grid=(starts[-1]...  15.9 us
    ppermute x1, waiting for transfers between devices, local(): far = lax.ppermute(far, 'pair', back)  14.2 us
    ppermute x1, starting transfers between devices, local(): far = lax.ppermute(far, 'pair', back)  10.6 us
    ppermute x8, waiting for transfers between devices, local(): moved = lax.ppermute(sent, 'pair', ahead if way == 'up' else behind)  10.5 us
  transfers between devices with their start and end apart: 17, of which 5 were waited for; matrix products, arithmetic and copies ran while one was open for 1% of the time, Pallas kernels for 15%

profile of v2, /device:TPU:97, one launch (start us, length us, event | category | flops | bytes accessed | tf_op | source)
XLA Modules:
  0.0 195.2 jit_solution(5535525711374637778)
XLA Ops:
  0.0 0.7 convert_bitcast_fusion
  0.7 0.7 copy.3.live_ref
  1.4 4.4 %whiten.2 = (bf16[8,2,128,256]{3,2,1,0:T(8,128)(2,1)}, bf16[8,2,128,256]{3,2,1,0:T(8,128)(2,1)}) custom-call(bf16[2,64,128,256]{3,2,1,0:T(8,128)(2,1)} %x_ref.2, f32[128,1]{1,0:T(8,128)} %copy.3.live_ref), custom_call_target="tpu_custom_call" | custom-call | flops 8388608 | bytes 4194304 | tf_op jit(solution)/shard_map/whiten/pallas_call | solution.py:60
  5.8 3.4 %collective-permute-start.1 = (bf16[8,2,128,256]{3,2,1,0:T(8,128)(2,1)}, bf16[8,2,128,256]{3,2,1,0:T(8,128)(2,1)S(1)}, u32[]{:S(2)}, u32[]{:S(2)}) collective-permute-start(bf16[8,2,128,256]{3,2,1,0:T(8,128)(2,1)} %get-tuple-element.30.refs_3_), channel_id=1, source_target_pairs={{0,40},{8,32},{16,24},{24,80},{32,72},{40,64},{48,56},{56,112},{64... | collective-permute-start | bytes 3145736 | tf_op jit(solution)/shard_map/ppermute | solution.py:226
  9.3 1.7 collective-permute-start.2
  10.9 0.5 collective-permute-start
  11.4 11.5 %whiten.3 = (bf16[8,2,128,256]{3,2,1,0:T(8,128)(2,1)}, bf16[8,2,128,256]{3,2,1,0:T(8,128)(2,1)}, bf16[8,2,128,256]{3,2,1,0:T(8,128)(2,1)}, bf16[8,2,128,256]{3,2...) custom-call(bf16[2,64,128,256]{3,2,1,0:T(8,128)(2,1)} %x_ref.2, f32[128,1]{1,0:T(8,128)} %copy.3.live_ref), custom_call_target="tpu_custom_call" | custom-call | flops 25165824 | bytes 12582912 | tf_op jit(solution)/shard_map/whiten/pallas_call | solution.py:60
  22.9 6.4 %collective-permute-start.5 = (bf16[8,2,128,256]{3,2,1,0:T(8,128)(2,1)}, bf16[8,2,128,256]{3,2,1,0:T(8,128)(2,1)}, u32[]{:S(2)}, u32[]{:S(2)}) collective-permute-start(bf16[8,2,128,256]{3,2,1,0:T(8,128)(2,1)} %get-tuple-element.37.refs_1_), channel_id=1, source_target_pairs={{0,40},{8,32},{16,24},{24,80},{32,72},{40,64},{48,56},{56,112},{64... | collective-permute-start | bytes 3145736 | tf_op jit(solution)/shard_map/ppermute | solution.py:226
  29.3 0.0 collective-permute-start.6
  29.4 0.1 iota_add_fusion
  29.4 0.1 iota_add_fusion.1
  29.5 0.1 iota_add_fusion.2
  29.6 0.1 iota_add_fusion.3
  29.7 0.1 iota_add_fusion.4
  29.7 0.1 iota_add_fusion.5
  29.8 0.1 iota_add_fusion.6
  29.9 0.1 iota_add_fusion.7
  29.9 2.2 %cosine_convert_fusion.2 = (bf16[8,1,8,256]{3,2,1,0:T(8,128)(2,1)S(1)}, bf16[8,1,8,256]{3,2,1,0:T(8,128)(2,1)S(1)}, bf16[8,1,8,256]{3,2,1,0:T(8,128)(2,1)S(1)}, ...) fusion(s32[256]{0:T(256)S(1)} %iota_add_fusion.8, ...), kind=kLoop, calls=%fused_computation.79 | loop fusion | flops 2228224 | bytes 527360 | tf_op jit(solution)/shard_map/convert.5
  32.3 0.2 collective-permute-done.1.refs_2_
  32.5 1.7 collective-permute-start.7
  34.2 0.0 collective-permute-done.2.refs_4_
  34.2 7.4 %collective-permute-start.8 = (bf16[8,2,128,256]{3,2,1,0:T(8,128)(2,1)}, bf16[8,2,128,256]{3,2,1,0:T(8,128)(2,1)}, u32[]{:S(2)}, u32[]{:S(2)}) collective-permute-start(bf16[8,2,128,256]{3,2,1,0:T(8,128)(2,1)} %get-tuple-element.40.refs_4_), channel_id=1, source_target_pairs={{0,40},{8,32},{16,24},{24,80},{32,72},{40,64},{48,56},{56,112},{64... | collective-permute-start | bytes 3145736 | tf_op jit(solution)/shard_map/ppermute | solution.py:226
  41.6 1.6 collective-permute-start.9
  43.2 0.7 copy-done.6
  44.0 3.8 %cross.5 = bf16[8,512,128]{2,1,0:T(8,128)(2,1)} custom-call(s32[1]{0:T(128)} %bitcast.pick_ref, bf16[8,2,128,256]{3,2,1,0:T(8,128)(2,1)S(1)} %copy-done, bf16[8,2,128,256]{3,2,1,0:T(8,128)(2,1)} %collective-permute-done.refs_1_, bf16[8,2,128,256]{3,2,1,0:T(8,128)(2,1)S(1)} %collective-permute-done.1.refs_2_, bf16[8,2,128,256]{3,2,1,0:T(8,128)(2,1)S(1)} %copy-done.1, ...), custom_call_target="tpu_custom_call" | custom-call | flops 536870912 | bytes 5242880 | tf_op jit(solution)/shard_map/cross/pallas_call | solution.py:116
  47.8 20.3 %all-to-all-start = ((bf16[8,512,128]{2,1,0:T(8,128)(2,1)}), bf16[8,512,128]{2,1,0:T(8,128)(2,1)S(1)}, u32[]{:S(2)}, u32[]{:S(2)}) async-start(bf16[8,512,128]{2,1,0:T(8,128)(2,1)} %cross.5), calls=%async_computation | async-start | bytes 2097152 | tf_op jit(solution)/shard_map/all_to_all | solution.py:237
  68.1 6.4 %collective-permute-start.4 = (bf16[8,2,128,256]{3,2,1,0:T(8,128)(2,1)S(1)}, bf16[8,2,128,256]{3,2,1,0:T(8,128)(2,1)}, u32[]{:S(2)}, u32[]{:S(2)}) collective-permute-start(bf16[8,2,128,256]{3,2,1,0:T(8,128)(2,1)S(1)} %copy-done.3), channel_id=1, source_target_pairs={{0,40},{8,32},{16,24},{24,80},{32,72},{40,64},{48,56},{56,112},{64... | collective-permute-start | bytes 3145736 | tf_op jit(solution)/shard_map/ppermute | solution.py:226
  74.5 1.7 collective-permute-start.10
  76.2 1.3 collective-permute-done.8.refs_3_
  77.5 1.2 copy-done.5
  78.7 4.4 %cross.6 = bf16[8,512,128]{2,1,0:T(8,128)(2,1)} custom-call(s32[1]{0:T(128)} %bitcast.pick_ref, bf16[8,2,128,256]{3,2,1,0:T(8,128)(2,1)} %collective-permute-done.5.refs_0_, bf16[8,2,128,256]{3,2,1,0:T(8,128)(2,1)S(1)} %copy-done.4, bf16[8,2,128,256]{3,2,1,0:T(8,128)(2,1)} %collective-permute-done.7.refs_2_, ...), custom_call_target="tpu_custom_call" | custom-call | flops 536870912 | bytes 5242880 | tf_op jit(solution)/shard_map/cross/pallas_call | solution.py:116
  83.1 4.9 %all-to-all-done.refs_0_ = bf16[8,512,128]{2,1,0:T(8,128)(2,1)S(1)} async-done(((bf16[8,512,128]{2,1,0:T(8,128)(2,1)}), bf16[8,512,128]{2,1,0:T(8,128)(2,1)S(1)}, u32[]{:S(2)}, u32[]{:S(2)}) %all-to-all-start) | async-done | bytes 1048608 | tf_op jit(solution)/shard_map/all_to_all | solution.py:237
  88.0 4.2 %all-to-all-start.1 = ((bf16[8,512,128]{2,1,0:T(8,128)(2,1)}), bf16[8,512,128]{2,1,0:T(8,128)(2,1)S(1)}, u32[]{:S(2)}, u32[]{:S(2)}) async-start(bf16[8,512,128]{2,1,0:T(8,128)(2,1)} %cross.6), calls=%async_computation.1 | async-start | bytes 2097152 | tf_op jit(solution)/shard_map/all_to_all | solution.py:237
  92.2 22.7 %collective-permute-start.3 = (bf16[8,2,128,256]{3,2,1,0:T(8,128)(2,1)}, bf16[8,2,128,256]{3,2,1,0:T(8,128)(2,1)}, u32[]{:S(2)}, u32[]{:S(2)}) collective-permute-start(bf16[8,2,128,256]{3,2,1,0:T(8,128)(2,1)} %get-tuple-element.34.refs_1_), channel_id=1, source_target_pairs={{0,40},{8,32},{16,24},{24,80},{32,72},{40,64},{48,56},{56,112},{64... | collective-permute-start | bytes 3145736 | tf_op jit(solution)/shard_map/ppermute | solution.py:226
  114.9 1.7 collective-permute-start.11
  116.6 3.0 %cross.7 = bf16[8,256,128]{2,1,0:T(8,128)(2,1)} custom-call(s32[1]{0:T(128)} %bitcast.pick_ref, bf16[8,2,128,256]{3,2,1,0:T(8,128)(2,1)} %collective-permute-done.4.refs_0_, bf16[8,2,128,256]{3,2,1,0:T(8,128)(2,1)S(1)} %copy-done.3, bf16[8,2,128,256]{3,2,1,0:T(8,128)(2,1)} %collective-permute-done.10.refs_2_), custom_call_target="tpu_custom_call" | custom-call | flops 268435456 | bytes 2621440 | tf_op jit(solution)/shard_map/cross/pallas_call | solution.py:116
  119.6 5.4 %all-to-all-start.2 = ((bf16[8,256,128]{2,1,0:T(8,128)(2,1)}), bf16[8,256,128]{2,1,0:T(8,128)(2,1)S(1)}, u32[]{:S(2)}, u32[]{:S(2)}) async-start(bf16[8,256,128]{2,1,0:T(8,128)(2,1)} %cross.7), calls=%async_computation.2 | async-start | bytes 1048576 | tf_op jit(solution)/shard_map/all_to_all | solution.py:237
  125.0 9.0 %collective-permute-done.3.refs_0_ = bf16[8,2,128,256]{3,2,1,0:T(8,128)(2,1)} collective-permute-done((bf16[8,2,128,256]{3,2,1,0:T(8,128)(2,1)}, bf16[8,2,128,256]{3,2,1,0:T(8,128)(2,1)}, u32[]{:S(2)}, u32[]{:S(2)}) %collective-permute-start.3) | collective-permute-done | bytes 1048608 | tf_op jit(solution)/shard_map/ppermute | solution.py:226
  134.1 2.5 %cross.8 = bf16[8,256,128]{2,1,0:T(8,128)(2,1)S(1)} custom-call(s32[1]{0:T(128)} %bitcast.pick_ref, bf16[8,2,128,256]{3,2,1,0:T(8,128)(2,1)} %collective-permute-done.3.refs_0_, bf16[8,2,128,256]{3,2,1,0:T(8,128)(2,1)} %get-tuple-element.34.refs_1_, bf16[8,2,128,256]{3,2,1,0:T(8,128)(2,1)} %collective-permute-done.11.refs_2_), custom_call_target="tpu_custom_call" | custom-call | flops 268435456 | bytes 2621440 | tf_op jit(solution)/shard_map/cross/pallas_call | solution.py:116
  136.6 13.2 %all_to_all.25.refs_4_ = bf16[8,256,128]{2,1,0:T(8,128)(2,1)S(1)} all-to-all(bf16[8,256,128]{2,1,0:T(8,128)(2,1)S(1)} %cross.8), channel_id=1, replica_groups=mesh['pair'=32,'band'=8] {'band'}, dimensions={0} | all-to-all | bytes 1048576 | tf_op jit(solution)/shard_map/all_to_all | solution.py:237
  149.9 1.0 copy-done.7
  150.9 1.0 to_lags.3
  151.9 10.6 %collective-permute-start.13 = (bf16[2048,256]{1,0:T(8,128)(2,1)S(1)}, bf16[2048,256]{1,0:T(8,128)(2,1)S(1)}, u32[]{:S(2)}, u32[]{:S(2)}) collective-permute-start(bf16[2048,256]{1,0:T(8,128)(2,1)S(1)} %to_lags.3), channel_id=1, source_target_pairs={{40,0},{32,8},{24,16},{80,24},{72,32},{64,40},{56,48},{112,56},{10... | collective-permute-start | bytes 3145736 | tf_op jit(solution)/shard_map/ppermute | solution.py:246
  162.5 3.1 %cross.9 = bf16[8,512,128]{2,1,0:T(8,128)(2,1)S(1)} custom-call(s32[1]{0:T(128)} %bitcast.pick_ref, bf16[8,2,128,256]{3,2,1,0:T(8,128)(2,1)S(1)} %copy-done.2, bf16[8,2,128,256]{3,2,1,0:T(8,128)(2,1)} %collective-permute-done.6.refs_1_, bf16[8,2,128,256]{3,2,1,0:T(8,128)(2,1)} %get-tuple-element.48.refs_2_, ...), custom_call_target="tpu_custom_call" | custom-call | flops 536870912 | bytes 5242880 | tf_op jit(solution)/shard_map/cross/pallas_call | solution.py:116
  165.6 13.1 %all_to_all.26.refs_1_.refs_2_ = bf16[8,512,128]{2,1,0:T(8,128)(2,1)S(1)} all-to-all(bf16[8,512,128]{2,1,0:T(8,128)(2,1)S(1)} %cross.9), channel_id=1, replica_groups=mesh['pair'=32,'band'=8] {'band'}, dimensions={0} | all-to-all | bytes 2097152 | tf_op jit(solution)/shard_map/all_to_all | solution.py:237
  178.7 0.8 to_lags.2
  179.5 14.2 %collective-permute-done.13 = bf16[2048,256]{1,0:T(8,128)(2,1)S(1)} collective-permute-done((bf16[2048,256]{1,0:T(8,128)(2,1)S(1)}, bf16[2048,256]{1,0:T(8,128)(2,1)S(1)}, u32[]{:S(2)}, u32[]{:S(2)}) %collective-permute-start.13) | collective-permute-done | bytes 1048608 | tf_op jit(solution)/shard_map/ppermute | solution.py:246
  193.7 1.5 convert_add_fusion
  (44 shorter events, 0.2 us)
Async XLA Ops:
  5.8 26.7 %collective-permute-start.1 = (bf16[8,2,128,256]{3,2,1,0:T(8,128)(2,1)}, bf16[8,2,128,256]{3,2,1,0:T(8,128)(2,1)S(1)}, u32[]{:S(2)}, u32[]{:S(2)}) collective-permute-start(bf16[8,2,128,256]{3,2,1,0:T(8,128)(2,1)} %get-tuple-element.30.refs_3_), channel_id=1, source_target_pairs={{0,40},{8,32},{16,24},{24,80},{32,72},{40,64},{48,56},{56,112},{64... | collective-permute-start | bytes 3145736 | tf_op jit(solution)/shard_map/ppermute | solution.py:226
  9.3 24.9 %collective-permute-start.2 = (bf16[8,2,128,256]{3,2,1,0:T(8,128)(2,1)}, bf16[8,2,128,256]{3,2,1,0:T(8,128)(2,1)}, u32[]{:S(2)}, u32[]{:S(2)}) collective-permute-start(bf16[8,2,128,256]{3,2,1,0:T(8,128)(2,1)} %get-tuple-element.30.refs_3_), channel_id=1, source_target_pairs={{48,32},{56,24},{64,80},{80,64},{88,56},{96,112},{112,96},{120,88}... | collective-permute-start | bytes 3145736 | tf_op jit(solution)/shard_map/ppermute | solution.py:229
  10.9 30.6 %collective-permute-start = (bf16[8,2,128,256]{3,2,1,0:T(8,128)(2,1)}, bf16[8,2,128,256]{3,2,1,0:T(8,128)(2,1)}, u32[]{:S(2)}, u32[]{:S(2)}) collective-permute-start(bf16[8,2,128,256]{3,2,1,0:T(8,128)(2,1)} %get-tuple-element.29.refs_0_), channel_id=1, source_target_pairs={{40,0},{48,8},{56,16},{64,24},{72,32},{80,40},{88,48},{96,56},{104... | collective-permute-start | bytes 3145736 | tf_op jit(solution)/shard_map/ppermute | solution.py:226
  22.9 21.1 %copy-start = (bf16[8,2,128,256]{3,2,1,0:T(8,128)(2,1)S(1)}, bf16[8,2,128,256]{3,2,1,0:T(8,128)(2,1)}, u32[]{:S(2)}) copy-start(bf16[8,2,128,256]{3,2,1,0:T(8,128)(2,1)} %get-tuple-element.29.refs_0_) | copy-start | bytes 3145732
  22.9 21.1 %copy-start.1 = (bf16[8,2,128,256]{3,2,1,0:T(8,128)(2,1)S(1)}, bf16[8,2,128,256]{3,2,1,0:T(8,128)(2,1)}, u32[]{:S(2)}) copy-start(bf16[8,2,128,256]{3,2,1,0:T(8,128)(2,1)} %get-tuple-element.30.refs_3_) | copy-start | bytes 3145732
  22.9 45.2 %collective-permute-start.5 = (bf16[8,2,128,256]{3,2,1,0:T(8,128)(2,1)}, bf16[8,2,128,256]{3,2,1,0:T(8,128)(2,1)}, u32[]{:S(2)}, u32[]{:S(2)}) collective-permute-start(bf16[8,2,128,256]{3,2,1,0:T(8,128)(2,1)} %get-tuple-element.37.refs_1_), channel_id=1, source_target_pairs={{0,40},{8,32},{16,24},{24,80},{32,72},{40,64},{48,56},{56,112},{64... | collective-permute-start | bytes 3145736 | tf_op jit(solution)/shard_map/ppermute | solution.py:226
  29.3 45.2 %collective-permute-start.6 = (bf16[8,2,128,256]{3,2,1,0:T(8,128)(2,1)}, bf16[8,2,128,256]{3,2,1,0:T(8,128)(2,1)}, u32[]{:S(2)}, u32[]{:S(2)}) collective-permute-start(bf16[8,2,128,256]{3,2,1,0:T(8,128)(2,1)} %get-tuple-element.46.refs_0_), channel_id=1, source_target_pairs={{40,0},{48,8},{56,16},{64,24},{72,32},{80,40},{88,48},{96,56},{104... | collective-permute-start | bytes 3145736 | tf_op jit(solution)/shard_map/ppermute | solution.py:226
  32.5 43.7 %collective-permute-start.7 = (bf16[8,2,128,256]{3,2,1,0:T(8,128)(2,1)}, bf16[8,2,128,256]{3,2,1,0:T(8,128)(2,1)}, u32[]{:S(2)}, u32[]{:S(2)}) collective-permute-start(bf16[8,2,128,256]{3,2,1,0:T(8,128)(2,1)} %get-tuple-element.37.refs_1_), channel_id=1, source_target_pairs={{48,32},{56,24},{64,80},{80,64},{88,56},{96,112},{112,96},{120,88}... | collective-permute-start | bytes 3145736 | tf_op jit(solution)/shard_map/ppermute | solution.py:229
  34.2 43.3 %collective-permute-start.8 = (bf16[8,2,128,256]{3,2,1,0:T(8,128)(2,1)}, bf16[8,2,128,256]{3,2,1,0:T(8,128)(2,1)}, u32[]{:S(2)}, u32[]{:S(2)}) collective-permute-start(bf16[8,2,128,256]{3,2,1,0:T(8,128)(2,1)} %get-tuple-element.40.refs_4_), channel_id=1, source_target_pairs={{0,40},{8,32},{16,24},{24,80},{32,72},{40,64},{48,56},{56,112},{64... | collective-permute-start | bytes 3145736 | tf_op jit(solution)/shard_map/ppermute | solution.py:226
  41.6 35.9 %collective-permute-start.9 = (bf16[8,2,128,256]{3,2,1,0:T(8,128)(2,1)}, bf16[8,2,128,256]{3,2,1,0:T(8,128)(2,1)}, u32[]{:S(2)}, u32[]{:S(2)}) collective-permute-start(bf16[8,2,128,256]{3,2,1,0:T(8,128)(2,1)} %get-tuple-element.40.refs_4_), channel_id=1, source_target_pairs={{48,32},{56,24},{64,80},{80,64},{88,56},{96,112},{112,96},{120,88}... | collective-permute-start | bytes 3145736 | tf_op jit(solution)/shard_map/ppermute | solution.py:229
  43.2 0.7 copy-start.6
  47.8 20.3 %copy-start.3 = (bf16[8,2,128,256]{3,2,1,0:T(8,128)(2,1)S(1)}, bf16[8,2,128,256]{3,2,1,0:T(8,128)(2,1)}, u32[]{:S(2)}) copy-start(bf16[8,2,128,256]{3,2,1,0:T(8,128)(2,1)} %get-tuple-element.36.refs_1_) | copy-start | bytes 3145732
  47.8 29.7 %copy-start.4 = (bf16[8,2,128,256]{3,2,1,0:T(8,128)(2,1)S(1)}, bf16[8,2,128,256]{3,2,1,0:T(8,128)(2,1)}, u32[]{:S(2)}) copy-start(bf16[8,2,128,256]{3,2,1,0:T(8,128)(2,1)} %get-tuple-element.37.refs_1_) | copy-start | bytes 3145732
  47.8 40.2 %all-to-all-start = ((bf16[8,512,128]{2,1,0:T(8,128)(2,1)}), bf16[8,512,128]{2,1,0:T(8,128)(2,1)S(1)}, u32[]{:S(2)}, u32[]{:S(2)}) async-start(bf16[8,512,128]{2,1,0:T(8,128)(2,1)} %cross.5), calls=%async_computation | async-start | bytes 2097152 | tf_op jit(solution)/shard_map/all_to_all | solution.py:237
  68.1 48.5 %collective-permute-start.4 = (bf16[8,2,128,256]{3,2,1,0:T(8,128)(2,1)S(1)}, bf16[8,2,128,256]{3,2,1,0:T(8,128)(2,1)}, u32[]{:S(2)}, u32[]{:S(2)}) collective-permute-start(bf16[8,2,128,256]{3,2,1,0:T(8,128)(2,1)S(1)} %copy-done.3), channel_id=1, source_target_pairs={{0,40},{8,32},{16,24},{24,80},{32,72},{40,64},{48,56},{56,112},{64... | collective-permute-start | bytes 3145736 | tf_op jit(solution)/shard_map/ppermute | solution.py:226
  74.5 42.1 %collective-permute-start.10 = (bf16[8,2,128,256]{3,2,1,0:T(8,128)(2,1)S(1)}, bf16[8,2,128,256]{3,2,1,0:T(8,128)(2,1)}, u32[]{:S(2)}, u32[]{:S(2)}) collective-permute-start(bf16[8,2,128,256]{3,2,1,0:T(8,128)(2,1)S(1)} %copy-done.3), channel_id=1, source_target_pairs={{48,32},{56,24},{64,80},{80,64},{88,56},{96,112},{112,96},{120,88}... | collective-permute-start | bytes 3145736 | tf_op jit(solution)/shard_map/ppermute | solution.py:229
  77.5 1.2 copy-start.5
  88.0 31.6 %all-to-all-start.1 = ((bf16[8,512,128]{2,1,0:T(8,128)(2,1)}), bf16[8,512,128]{2,1,0:T(8,128)(2,1)S(1)}, u32[]{:S(2)}, u32[]{:S(2)}) async-start(bf16[8,512,128]{2,1,0:T(8,128)(2,1)} %cross.6), calls=%async_computation.1 | async-start | bytes 2097152 | tf_op jit(solution)/shard_map/all_to_all | solution.py:237
  92.2 41.9 %collective-permute-start.3 = (bf16[8,2,128,256]{3,2,1,0:T(8,128)(2,1)}, bf16[8,2,128,256]{3,2,1,0:T(8,128)(2,1)}, u32[]{:S(2)}, u32[]{:S(2)}) collective-permute-start(bf16[8,2,128,256]{3,2,1,0:T(8,128)(2,1)} %get-tuple-element.34.refs_1_), channel_id=1, source_target_pairs={{0,40},{8,32},{16,24},{24,80},{32,72},{40,64},{48,56},{56,112},{64... | collective-permute-start | bytes 3145736 | tf_op jit(solution)/shard_map/ppermute | solution.py:226
  114.9 19.2 %collective-permute-start.11 = (bf16[8,2,128,256]{3,2,1,0:T(8,128)(2,1)}, bf16[8,2,128,256]{3,2,1,0:T(8,128)(2,1)}, u32[]{:S(2)}, u32[]{:S(2)}) collective-permute-start(bf16[8,2,128,256]{3,2,1,0:T(8,128)(2,1)} %get-tuple-element.34.refs_1_), channel_id=1, source_target_pairs={{48,32},{56,24},{64,80},{80,64},{88,56},{96,112},{112,96},{120,88}... | collective-permute-start | bytes 3145736 | tf_op jit(solution)/shard_map/ppermute | solution.py:229
  116.6 45.9 %collective-permute-start.12 = (bf16[8,2,128,256]{3,2,1,0:T(8,128)(2,1)}, bf16[8,2,128,256]{3,2,1,0:T(8,128)(2,1)}, u32[]{:S(2)}, u32[]{:S(2)}) collective-permute-start(bf16[8,2,128,256]{3,2,1,0:T(8,128)(2,1)} %get-tuple-element.48.refs_2_), channel_id=1, source_target_pairs={{40,0},{48,8},{56,16},{64,24},{72,32},{80,40},{88,48},{96,56},{104... | collective-permute-start | bytes 3145736 | tf_op jit(solution)/shard_map/ppermute | solution.py:226
  119.6 17.0 %all-to-all-start.2 = ((bf16[8,256,128]{2,1,0:T(8,128)(2,1)}), bf16[8,256,128]{2,1,0:T(8,128)(2,1)S(1)}, u32[]{:S(2)}, u32[]{:S(2)}) async-start(bf16[8,256,128]{2,1,0:T(8,128)(2,1)} %cross.7), calls=%async_computation.2 | async-start | bytes 1048576 | tf_op jit(solution)/shard_map/all_to_all | solution.py:237
  149.9 1.0 copy-start.7
  150.9 11.6 %copy-start.2 = (bf16[8,2,128,256]{3,2,1,0:T(8,128)(2,1)S(1)}, bf16[8,2,128,256]{3,2,1,0:T(8,128)(2,1)}, u32[]{:S(2)}) copy-start(bf16[8,2,128,256]{3,2,1,0:T(8,128)(2,1)} %get-tuple-element.46.refs_0_) | copy-start | bytes 3145732
  151.9 41.8 %collective-permute-start.13 = (bf16[2048,256]{1,0:T(8,128)(2,1)S(1)}, bf16[2048,256]{1,0:T(8,128)(2,1)S(1)}, u32[]{:S(2)}, u32[]{:S(2)}) collective-permute-start(bf16[2048,256]{1,0:T(8,128)(2,1)S(1)} %to_lags.3), channel_id=1, source_target_pairs={{40,0},{32,8},{24,16},{80,24},{72,32},{64,40},{56,48},{112,56},{10... | collective-permute-start | bytes 3145736 | tf_op jit(solution)/shard_map/ppermute | solution.py:246

commit v3 on v2

--- a/solution.py
+++ b/solution.py
@@ -11,19 +11,24 @@
 NFFT = 2048
 K0 = 64
 OFFSET = 5
-STEP = 4
+STEP = 8
 GROUPS = (("down", 1), ("up", 1), ("up", 1), ("down", 1), ("up", 1), ("up", 1), ("down", 1), ("up", 1))
-WHITEN = (2, 6)
+WHITEN = (2, 3, 3)
 PLAN = (
     ("send", 0),
     ("send", 1),
+    ("third", 1),
     ("send", 2),
+    ("third", 2),
     ("send", 3),
     ("send", 4),
+    ("third", 4),
     ("join", (0, 1), "t", "s"),
     ("send", 5, "v0"),
+    ("third", 5, "v0"),
     ("join", (2, 4), "v0", "g3"),
     ("send", 7, "p0"),
+    ("third", 7, "p0"),
     ("send", 6, "g5"),
     ("join", (5,), "v1", "p0"),
     ("join", (7,), "v2", "p1"),
@@ -31,19 +36,32 @@
 )
 
 
+def row_sums(x):
+    ones = jnp.ones((x.shape[1], 128), jnp.bfloat16)
+    high = x.astype(jnp.bfloat16)
+    low = (x - high.astype(jnp.float32)).astype(jnp.bfloat16)
+    return jnp.dot(high, ones, preferred_element_type=jnp.float32) + jnp.dot(
+        low, ones, preferred_element_type=jnp.float32
+    )
+
+
 def whiten_kernel(starts, x_ref, live_ref, *o_refs):
-    live = live_ref[...]
-    windows = x_ref.shape[3]
+    channels, windows = x_ref.shape[2:]
     step = pl.program_id(0)
+    rows = lax.broadcasted_iota(jnp.int32, (channels, channels), 0)
+    columns = lax.broadcasted_iota(jnp.int32, (channels, channels), 1)
+    live = row_sums(jnp.where(rows == columns, live_ref[...].astype(jnp.float32), 0.0))
 
     def write(o_ref):
         for f in range(STEP):
             real = x_ref[0, f].astype(jnp.float32)
             imag = x_ref[1, f].astype(jnp.float32)
-            power = jnp.sum(real * real + imag * imag, axis=1, keepdims=True) * (1.0 / windows)
+            power = row_sums(real * real + imag * imag) * (1.0 / windows)
             scale = live * lax.rsqrt(live * live * power + 1e-06)
-            o_ref[f, 0] = (real * scale).astype(jnp.bfloat16)
-            o_ref[f, 1] = (imag * scale).astype(jnp.bfloat16)
+            for lane in range(0, windows, 128):
+                part = slice(lane, lane + 128)
+                o_ref[f, 0, :, part] = (real[:, part] * scale).astype(jnp.bfloat16)
+                o_ref[f, 1, :, part] = (imag[:, part] * scale).astype(jnp.bfloat16)
 
     for k, o_ref in enumerate(o_refs):
         pl.when((step >= starts[k]) & (step < starts[k + 1]))(functools.partial(write, o_ref))
@@ -62,7 +80,7 @@
         grid=(starts[-1],),
         in_specs=[
             pl.BlockSpec((2, STEP, channels, windows), lambda i: (0, first // STEP + i, 0, 0)),
-            pl.BlockSpec((channels, 1), lambda i: (0, 0)),
+            pl.BlockSpec((1, channels), lambda i: (0, 0)),
         ],
         out_specs=[
             pl.BlockSpec((STEP, 2, channels, windows), out_block(k)) for k in range(len(counts))
@@ -118,7 +136,7 @@
         in_specs=[pl.BlockSpec(memory_space=pltpu.SMEM)]
         + [pl.BlockSpec(memory_space=pltpu.VMEM)] * sum(1 + len(ys) for _, ys in groups),
         out_shape=jax.ShapeDtypeStruct((bands, sum(rows) // bands, channels), jnp.bfloat16),
-        scratch_shapes=[pltpu.VMEM((max(rows), channels), jnp.float32)],
+        scratch_shapes=[pltpu.VMEM((max(rows) + max(rows) // channels, channels), jnp.float32)],
         compiler_params=pltpu.CompilerParams(vmem_limit_bytes=40 * 1024 * 1024),
         cost_estimate=pl.CostEstimate(
             flops=4 * work * channels, bytes_accessed=5 * work, transcendentals=0
@@ -189,7 +207,7 @@
     bands = lax.axis_size("band")
     behind, ahead, third, back = routes(lax.axis_size("pair"))
     norm = 1.0 / float(freq_local * bands) ** 0.5
-    mask = live.astype(jnp.float32)[:, None]
+    mask = live[None, :]
     pick = (lax.axis_index("pair") % 4 != 1).astype(jnp.int32)[None]
     counts = [eighths * freq_local // 8 for _, eighths in GROUPS]
     firsts = [sum(counts[:k]) for k in range(len(counts))]
@@ -218,21 +236,24 @@
     arrived = {}
     pieces = {"up": [], "down": []}
     for kind, what, *needs in PLAN:
-        if kind == "send":
+        if kind != "join":
             way, own = GROUPS[what][0], white[what]
             sent = own
             for need in needs:
                 sent = after(sent, there[need])
-            moved = lax.ppermute(sent, "pair", ahead if way == "up" else behind)
-            there[f"g{what}"] = moved
-            if way == "up":
-                arrived[what] = (moved, [own, lax.ppermute(sent, "pair", third)])
+            if kind == "third":
+                moved = there[f"y{what}"] = lax.ppermute(sent, "pair", third)
+                arrived.setdefault(what, [own, [own]])[1].append(moved)
+            elif way == "up":
+                moved = there[f"g{what}"] = lax.ppermute(sent, "pair", ahead)
+                arrived.setdefault(what, [own, [own]])[0] = moved
             else:
-                arrived[what] = (own, [moved])
+                moved = there[f"g{what}"] = lax.ppermute(sent, "pair", behind)
+                arrived[what] = [own, [moved]]
             continue
         factors = [arrived[k] for k in what]
         for need in needs:
-            factors[0] = (after(factors[0][0], there[need]), factors[0][1])
+            factors[0] = [after(factors[0][0], there[need]), factors[0][1]]
         value = cross(factors, pick, bands)
         piece = lax.all_to_all(value, "band", 0, 0)
         number = sum(name[0] == "v" for name in there)

time: 196 us -> 193 us (0.985)
  the two profiles are of different devices: /device:TPU:97 before, /device:TPU:1 now
where the time goes in v3:
time: 193 us; the launch traced here: 190 us
  starting transfers between devices  97.9 us (51%)
  Pallas kernels  34.2 us (18%)
  waiting for transfers between devices  25.7 us (13%)
  blocking collectives  25.6 us (13%)
  other arithmetic  4.47 us (2%)
    ppermute x5, starting transfers between devices, local(): moved = there[f'g{what}'] = lax.ppermute(sent, 'pair', ahead)  31.8 us
    all_to_all x2, blocking collectives, local(): piece = lax.all_to_all(value, 'band', 0, 0)  25.6 us
    ppermute x3, starting transfers between devices, local(): moved = there[f'g{what}'] = lax.ppermute(sent, 'pair', behind)  25 us
    ppermute x1, starting transfers between devices, local(): far = lax.ppermute(far, 'pair', back)  19.5 us
    pallas_call x5, Pallas kernels, cross(): pl.pallas_call(functools.partial(cross_kernel, [len(ys) for _, ys in grou...  16.9 us
    pallas_call x3, Pallas kernels, whiten(): pl.pallas_call(functools.partial(whiten_kernel, starts), grid=(starts[-1]...  15.6 us
    all_to_all x3, starting transfers between devices, local(): piece = lax.all_to_all(value, 'band', 0, 0)  13.2 us
    ppermute x3, waiting for transfers between devices, local(): moved = there[f'g{what}'] = lax.ppermute(sent, 'pair', behind)  12.5 us
  transfers between devices with their start and end apart: 17, of which 5 were waited for; matrix products, arithmetic and copies ran while one was open for 2% of the time, Pallas kernels for 16%

profile of v3, /device:TPU:1, one launch (start us, length us, event | category | flops | bytes accessed | tf_op | source)
XLA Modules:
  0.0 190.0 jit_solution(12027833670482753628)
XLA Ops:
  0.0 4.1 %whiten.3 = (bf16[8,2,128,256]{3,2,1,0:T(8,128)(2,1)}, bf16[8,2,128,256]{3,2,1,0:T(8,128)(2,1)}) custom-call(bf16[2,64,128,256]{3,2,1,0:T(8,128)(2,1)} %x_ref.3, s32[1,128]{1,0:T(1,128)} %bitcast.18), custom_call_target="tpu_custom_call" | custom-call | flops 8388608 | bytes 4194304 | tf_op jit(solution)/shard_map/whiten/pallas_call | solution.py:78
  4.1 3.0 %collective-permute-start.1 = (bf16[8,2,128,256]{3,2,1,0:T(8,128)(2,1)}, bf16[8,2,128,256]{3,2,1,0:T(8,128)(2,1)S(1)}, u32[]{:S(2)}, u32[]{:S(2)}) collective-permute-start(bf16[8,2,128,256]{3,2,1,0:T(8,128)(2,1)} %get-tuple-element.31.refs_3_), channel_id=1, source_target_pairs={{0,40},{8,32},{16,24},{24,80},{32,72},{40,64},{48,56},{56,112},{64... | collective-permute-start | bytes 3145736 | tf_op jit(solution)/shard_map/ppermute | solution.py:248
  7.1 1.6 collective-permute-start.2
  8.8 7.5 %collective-permute-start = (bf16[8,2,128,256]{3,2,1,0:T(8,128)(2,1)}, bf16[8,2,128,256]{3,2,1,0:T(8,128)(2,1)}, u32[]{:S(2)}, u32[]{:S(2)}) collective-permute-start(bf16[8,2,128,256]{3,2,1,0:T(8,128)(2,1)} %get-tuple-element.30.refs_0_), channel_id=1, source_target_pairs={{40,0},{48,8},{56,16},{64,24},{72,32},{80,40},{88,48},{96,56},{104... | collective-permute-start | bytes 3145736 | tf_op jit(solution)/shard_map/ppermute | solution.py:251
  16.2 5.7 %whiten.4 = (bf16[8,2,128,256]{3,2,1,0:T(8,128)(2,1)}, bf16[8,2,128,256]{3,2,1,0:T(8,128)(2,1)}, bf16[8,2,128,256]{3,2,1,0:T(8,128)(2,1)}) custom-call(bf16[2,64,128,256]{3,2,1,0:T(8,128)(2,1)} %x_ref.3, s32[1,128]{1,0:T(1,128)} %bitcast.19), custom_call_target="tpu_custom_call" | custom-call | flops 12582912 | bytes 6291456 | tf_op jit(solution)/shard_map/whiten/pallas_call | solution.py:78
  21.9 1.1 collective-permute-start.5
  23.0 1.9 collective-permute-start.6
  25.0 0.1 iota_add_fusion
  25.0 0.1 iota_add_fusion.1
  25.1 0.1 iota_add_fusion.2
  25.2 0.1 iota_add_fusion.3
  25.2 0.1 iota_add_fusion.4
  25.3 0.1 iota_add_fusion.5
  25.4 0.1 iota_add_fusion.6
  25.5 0.1 iota_add_fusion.7
  25.5 2.2 %cosine_convert_fusion.2 = (bf16[8,1,8,256]{3,2,1,0:T(8,128)(2,1)S(1)}, bf16[8,1,8,256]{3,2,1,0:T(8,128)(2,1)S(1)}, bf16[8,1,8,256]{3,2,1,0:T(8,128)(2,1)S(1)}, ...) fusion(s32[256]{0:T(256)S(1)} %iota_add_fusion.8, ...), kind=kLoop, calls=%fused_computation.79 | loop fusion | flops 2228224 | bytes 527360 | tf_op jit(solution)/shard_map/convert.5
  27.9 7.5 %collective-permute-done.1.refs_2_ = bf16[8,2,128,256]{3,2,1,0:T(8,128)(2,1)S(1)} collective-permute-done((bf16[8,2,128,256]{3,2,1,0:T(8,128)(2,1)}, bf16[8,2,128,256]{3,2,1,0:T(8,128)(2,1)S(1)}, u32[]{:S(2)}, u32[]{:S(2)}) %collective-permute-start.1) | collective-permute-done | bytes 1048608 | tf_op jit(solution)/shard_map/ppermute | solution.py:248
  35.4 0.0 collective-permute-start.8
  35.4 0.0 collective-permute-done.2.refs_4_
  35.4 1.7 collective-permute-start.9
  37.0 10.3 %collective-permute-done.refs_1_ = bf16[8,2,128,256]{3,2,1,0:T(8,128)(2,1)} collective-permute-done((bf16[8,2,128,256]{3,2,1,0:T(8,128)(2,1)}, bf16[8,2,128,256]{3,2,1,0:T(8,128)(2,1)}, u32[]{:S(2)}, u32[]{:S(2)}) %collective-permute-start) | collective-permute-done | bytes 1048608 | tf_op jit(solution)/shard_map/ppermute | solution.py:251
  47.3 1.7 collective-permute-start.7
  49.0 0.7 copy-done.6
  49.8 3.8 %cross.5 = bf16[8,512,128]{2,1,0:T(8,128)(2,1)} custom-call(s32[1]{0:T(128)} %bitcast.pick_ref, bf16[8,2,128,256]{3,2,1,0:T(8,128)(2,1)S(1)} %copy-done, bf16[8,2,128,256]{3,2,1,0:T(8,128)(2,1)} %collective-permute-done.refs_1_, bf16[8,2,128,256]{3,2,1,0:T(8,128)(2,1)S(1)} %collective-permute-done.1.refs_2_, bf16[8,2,128,256]{3,2,1,0:T(8,128)(2,1)S(1)} %copy-done.1, ...), custom_call_target="tpu_custom_call" | custom-call | flops 536870912 | bytes 5242880 | tf_op jit(solution)/shard_map/cross/pallas_call | solution.py:134
  53.6 4.1 %all-to-all-start = ((bf16[8,512,128]{2,1,0:T(8,128)(2,1)}), bf16[8,512,128]{2,1,0:T(8,128)(2,1)S(1)}, u32[]{:S(2)}, u32[]{:S(2)}) async-start(bf16[8,512,128]{2,1,0:T(8,128)(2,1)} %cross.5), calls=%async_computation | async-start | bytes 2097152 | tf_op jit(solution)/shard_map/all_to_all | solution.py:258
  57.7 5.8 %whiten.5 = (bf16[8,2,128,256]{3,2,1,0:T(8,128)(2,1)}, bf16[8,2,128,256]{3,2,1,0:T(8,128)(2,1)}, bf16[8,2,128,256]{3,2,1,0:T(8,128)(2,1)}) custom-call(bf16[2,64,128,256]{3,2,1,0:T(8,128)(2,1)} %x_ref.3, s32[1,128]{1,0:T(1,128)} %bitcast.20), custom_call_target="tpu_custom_call" | custom-call | flops 12582912 | bytes 6291456 | tf_op jit(solution)/shard_map/whiten/pallas_call | solution.py:78
  63.5 0.0 collective-permute-done.5.refs_0_
  63.5 16.8 %collective-permute-start.4 = (bf16[8,2,128,256]{3,2,1,0:T(8,128)(2,1)}, bf16[8,2,128,256]{3,2,1,0:T(8,128)(2,1)}, u32[]{:S(2)}, u32[]{:S(2)}) collective-permute-start(bf16[8,2,128,256]{3,2,1,0:T(8,128)(2,1)} %get-tuple-element.39.refs_1_), channel_id=1, source_target_pairs={{0,40},{8,32},{16,24},{24,80},{32,72},{40,64},{48,56},{56,112},{64... | collective-permute-start | bytes 3145736 | tf_op jit(solution)/shard_map/ppermute | solution.py:248
  80.4 2.2 %collective-permute-done.6.refs_1_ = bf16[8,2,128,256]{3,2,1,0:T(8,128)(2,1)} collective-permute-done((bf16[8,2,128,256]{3,2,1,0:T(8,128)(2,1)}, bf16[8,2,128,256]{3,2,1,0:T(8,128)(2,1)}, u32[]{:S(2)}, u32[]{:S(2)}) %collective-permute-start.6) | collective-permute-done | bytes 1048608 | tf_op jit(solution)/shard_map/ppermute | solution.py:251
  82.6 1.7 collective-permute-start.10
  84.3 4.5 %cross.6 = bf16[8,512,128]{2,1,0:T(8,128)(2,1)} custom-call(s32[1]{0:T(128)} %bitcast.pick_ref, bf16[8,2,128,256]{3,2,1,0:T(8,128)(2,1)} %collective-permute-done.5.refs_0_, bf16[8,2,128,256]{3,2,1,0:T(8,128)(2,1)S(1)} %copy-done.4, bf16[8,2,128,256]{3,2,1,0:T(8,128)(2,1)} %collective-permute-done.7.refs_2_, ...), custom_call_target="tpu_custom_call" | custom-call | flops 536870912 | bytes 5242880 | tf_op jit(solution)/shard_map/cross/pallas_call | solution.py:134
  88.7 4.3 %all-to-all-start.1 = ((bf16[8,512,128]{2,1,0:T(8,128)(2,1)}), bf16[8,512,128]{2,1,0:T(8,128)(2,1)S(1)}, u32[]{:S(2)}, u32[]{:S(2)}) async-start(bf16[8,512,128]{2,1,0:T(8,128)(2,1)} %cross.6), calls=%async_computation.1 | async-start | bytes 2097152 | tf_op jit(solution)/shard_map/all_to_all | solution.py:258
  93.0 10.9 %collective-permute-start.3 = (bf16[8,2,128,256]{3,2,1,0:T(8,128)(2,1)}, bf16[8,2,128,256]{3,2,1,0:T(8,128)(2,1)}, u32[]{:S(2)}, u32[]{:S(2)}) collective-permute-start(bf16[8,2,128,256]{3,2,1,0:T(8,128)(2,1)} %get-tuple-element.37.refs_1_), channel_id=1, source_target_pairs={{0,40},{8,32},{16,24},{24,80},{32,72},{40,64},{48,56},{56,112},{64... | collective-permute-start | bytes 3145736 | tf_op jit(solution)/shard_map/ppermute | solution.py:248
  103.9 1.7 collective-permute-start.11
  105.6 0.2 collective-permute-done.4.refs_0_
  105.8 15.6 %collective-permute-start.12 = (bf16[8,2,128,256]{3,2,1,0:T(8,128)(2,1)}, bf16[8,2,128,256]{3,2,1,0:T(8,128)(2,1)}, u32[]{:S(2)}, u32[]{:S(2)}) collective-permute-start(bf16[8,2,128,256]{3,2,1,0:T(8,128)(2,1)} %get-tuple-element.50.refs_2_), channel_id=1, source_target_pairs={{40,0},{48,8},{56,16},{64,24},{72,32},{80,40},{88,48},{96,56},{104... | collective-permute-start | bytes 3145736 | tf_op jit(solution)/shard_map/ppermute | solution.py:251
  121.4 3.0 %cross.7 = bf16[8,256,128]{2,1,0:T(8,128)(2,1)} custom-call(s32[1]{0:T(128)} %bitcast.pick_ref, bf16[8,2,128,256]{3,2,1,0:T(8,128)(2,1)} %collective-permute-done.4.refs_0_, bf16[8,2,128,256]{3,2,1,0:T(8,128)(2,1)S(1)} %copy-done.3, bf16[8,2,128,256]{3,2,1,0:T(8,128)(2,1)} %collective-permute-done.10.refs_2_), custom_call_target="tpu_custom_call" | custom-call | flops 268435456 | bytes 2621440 | tf_op jit(solution)/shard_map/cross/pallas_call | solution.py:134
  124.4 4.8 %all-to-all-start.2 = ((bf16[8,256,128]{2,1,0:T(8,128)(2,1)}), bf16[8,256,128]{2,1,0:T(8,128)(2,1)S(1)}, u32[]{:S(2)}, u32[]{:S(2)}) async-start(bf16[8,256,128]{2,1,0:T(8,128)(2,1)} %cross.7), calls=%async_computation.2 | async-start | bytes 1048576 | tf_op jit(solution)/shard_map/all_to_all | solution.py:258
  129.2 2.5 %cross.8 = bf16[8,256,128]{2,1,0:T(8,128)(2,1)S(1)} custom-call(s32[1]{0:T(128)} %bitcast.pick_ref, bf16[8,2,128,256]{3,2,1,0:T(8,128)(2,1)} %collective-permute-done.3.refs_0_, bf16[8,2,128,256]{3,2,1,0:T(8,128)(2,1)} %get-tuple-element.37.refs_1_, bf16[8,2,128,256]{3,2,1,0:T(8,128)(2,1)} %collective-permute-done.11.refs_2_), custom_call_target="tpu_custom_call" | custom-call | flops 268435456 | bytes 2621440 | tf_op jit(solution)/shard_map/cross/pallas_call | solution.py:134
  131.8 5.6 %all-to-all-done.2.refs_3_ = bf16[8,256,128]{2,1,0:T(8,128)(2,1)S(1)} async-done(((bf16[8,256,128]{2,1,0:T(8,128)(2,1)}), bf16[8,256,128]{2,1,0:T(8,128)(2,1)S(1)}, u32[]{:S(2)}, u32[]{:S(2)}) %all-to-all-start.2) | async-done | bytes 524320 | tf_op jit(solution)/shard_map/all_to_all | solution.py:258
  137.4 12.9 %all_to_all.25.refs_4_ = bf16[8,256,128]{2,1,0:T(8,128)(2,1)S(1)} all-to-all(bf16[8,256,128]{2,1,0:T(8,128)(2,1)S(1)} %cross.8), channel_id=1, replica_groups=mesh['pair'=32,'band'=8] {'band'}, dimensions={0} | all-to-all | bytes 1048576 | tf_op jit(solution)/shard_map/all_to_all | solution.py:258
  150.2 1.0 copy-done.7
  151.2 1.0 to_lags.3
  152.2 19.5 %collective-permute-start.13 = (bf16[2048,256]{1,0:T(8,128)(2,1)S(1)}, bf16[2048,256]{1,0:T(8,128)(2,1)S(1)}, u32[]{:S(2)}, u32[]{:S(2)}) collective-permute-start(bf16[2048,256]{1,0:T(8,128)(2,1)S(1)} %to_lags.3), channel_id=1, source_target_pairs={{40,0},{32,8},{24,16},{80,24},{72,32},{64,40},{56,48},{112,56},{10... | collective-permute-start | bytes 3145736 | tf_op jit(solution)/shard_map/ppermute | solution.py:267
  171.8 3.1 %cross.9 = bf16[8,512,128]{2,1,0:T(8,128)(2,1)S(1)} custom-call(s32[1]{0:T(128)} %bitcast.pick_ref, bf16[8,2,128,256]{3,2,1,0:T(8,128)(2,1)S(1)} %copy-done.2, bf16[8,2,128,256]{3,2,1,0:T(8,128)(2,1)} %collective-permute-done.6.refs_1_, bf16[8,2,128,256]{3,2,1,0:T(8,128)(2,1)} %get-tuple-element.50.refs_2_, ...), custom_call_target="tpu_custom_call" | custom-call | flops 536870912 | bytes 5242880 | tf_op jit(solution)/shard_map/cross/pallas_call | solution.py:134
  174.9 12.8 %all_to_all.26.refs_1_.refs_2_ = bf16[8,512,128]{2,1,0:T(8,128)(2,1)S(1)} all-to-all(bf16[8,512,128]{2,1,0:T(8,128)(2,1)S(1)} %cross.9), channel_id=1, replica_groups=mesh['pair'=32,'band'=8] {'band'}, dimensions={0} | all-to-all | bytes 2097152 | tf_op jit(solution)/shard_map/all_to_all | solution.py:258
  187.6 0.8 to_lags.2
  188.4 1.6 convert_add_fusion
  (43 shorter events, 0.2 us)
Async XLA Ops:
  4.1 31.3 %collective-permute-start.1 = (bf16[8,2,128,256]{3,2,1,0:T(8,128)(2,1)}, bf16[8,2,128,256]{3,2,1,0:T(8,128)(2,1)S(1)}, u32[]{:S(2)}, u32[]{:S(2)}) collective-permute-start(bf16[8,2,128,256]{3,2,1,0:T(8,128)(2,1)} %get-tuple-element.31.refs_3_), channel_id=1, source_target_pairs={{0,40},{8,32},{16,24},{24,80},{32,72},{40,64},{48,56},{56,112},{64... | collective-permute-start | bytes 3145736 | tf_op jit(solution)/shard_map/ppermute | solution.py:248
  7.1 28.2 %collective-permute-start.2 = (bf16[8,2,128,256]{3,2,1,0:T(8,128)(2,1)}, bf16[8,2,128,256]{3,2,1,0:T(8,128)(2,1)}, u32[]{:S(2)}, u32[]{:S(2)}) collective-permute-start(bf16[8,2,128,256]{3,2,1,0:T(8,128)(2,1)} %get-tuple-element.31.refs_3_), channel_id=1, source_target_pairs={{48,32},{56,24},{64,80},{80,64},{88,56},{96,112},{112,96},{120,88}... | collective-permute-start | bytes 3145736 | tf_op jit(solution)/shard_map/ppermute | solution.py:245
  8.8 38.6 %collective-permute-start = (bf16[8,2,128,256]{3,2,1,0:T(8,128)(2,1)}, bf16[8,2,128,256]{3,2,1,0:T(8,128)(2,1)}, u32[]{:S(2)}, u32[]{:S(2)}) collective-permute-start(bf16[8,2,128,256]{3,2,1,0:T(8,128)(2,1)} %get-tuple-element.30.refs_0_), channel_id=1, source_target_pairs={{40,0},{48,8},{56,16},{64,24},{72,32},{80,40},{88,48},{96,56},{104... | collective-permute-start | bytes 3145736 | tf_op jit(solution)/shard_map/ppermute | solution.py:251
  21.9 27.9 %copy-start = (bf16[8,2,128,256]{3,2,1,0:T(8,128)(2,1)S(1)}, bf16[8,2,128,256]{3,2,1,0:T(8,128)(2,1)}, u32[]{:S(2)}) copy-start(bf16[8,2,128,256]{3,2,1,0:T(8,128)(2,1)} %get-tuple-element.30.refs_0_) | copy-start | bytes 3145732
  21.9 27.9 %copy-start.1 = (bf16[8,2,128,256]{3,2,1,0:T(8,128)(2,1)S(1)}, bf16[8,2,128,256]{3,2,1,0:T(8,128)(2,1)}, u32[]{:S(2)}) copy-start(bf16[8,2,128,256]{3,2,1,0:T(8,128)(2,1)} %get-tuple-element.31.refs_3_) | copy-start | bytes 3145732
  21.9 41.6 %collective-permute-start.5 = (bf16[8,2,128,256]{3,2,1,0:T(8,128)(2,1)}, bf16[8,2,128,256]{3,2,1,0:T(8,128)(2,1)}, u32[]{:S(2)}, u32[]{:S(2)}) collective-permute-start(bf16[8,2,128,256]{3,2,1,0:T(8,128)(2,1)} %get-tuple-element.40.refs_1_), channel_id=1, source_target_pairs={{0,40},{8,32},{16,24},{24,80},{32,72},{40,64},{48,56},{56,112},{64... | collective-permute-start | bytes 3145736 | tf_op jit(solution)/shard_map/ppermute | solution.py:248
  23.0 59.6 %collective-permute-start.6 = (bf16[8,2,128,256]{3,2,1,0:T(8,128)(2,1)}, bf16[8,2,128,256]{3,2,1,0:T(8,128)(2,1)}, u32[]{:S(2)}, u32[]{:S(2)}) collective-permute-start(bf16[8,2,128,256]{3,2,1,0:T(8,128)(2,1)} %get-tuple-element.48.refs_0_), channel_id=1, source_target_pairs={{40,0},{48,8},{56,16},{64,24},{72,32},{80,40},{88,48},{96,56},{104... | collective-permute-start | bytes 3145736 | tf_op jit(solution)/shard_map/ppermute | solution.py:251
  35.4 48.9 %collective-permute-start.8 = (bf16[8,2,128,256]{3,2,1,0:T(8,128)(2,1)}, bf16[8,2,128,256]{3,2,1,0:T(8,128)(2,1)}, u32[]{:S(2)}, u32[]{:S(2)}) collective-permute-start(bf16[8,2,128,256]{3,2,1,0:T(8,128)(2,1)} %get-tuple-element.34.refs_4_), channel_id=1, source_target_pairs={{0,40},{8,32},{16,24},{24,80},{32,72},{40,64},{48,56},{56,112},{64... | collective-permute-start | bytes 3145736 | tf_op jit(solution)/shard_map/ppermute | solution.py:248
  35.4 48.9 %collective-permute-start.9 = (bf16[8,2,128,256]{3,2,1,0:T(8,128)(2,1)}, bf16[8,2,128,256]{3,2,1,0:T(8,128)(2,1)}, u32[]{:S(2)}, u32[]{:S(2)}) collective-permute-start(bf16[8,2,128,256]{3,2,1,0:T(8,128)(2,1)} %get-tuple-element.34.refs_4_), channel_id=1, source_target_pairs={{48,32},{56,24},{64,80},{80,64},{88,56},{96,112},{112,96},{120,88}... | collective-permute-start | bytes 3145736 | tf_op jit(solution)/shard_map/ppermute | solution.py:245
  47.3 36.9 %collective-permute-start.7 = (bf16[8,2,128,256]{3,2,1,0:T(8,128)(2,1)}, bf16[8,2,128,256]{3,2,1,0:T(8,128)(2,1)}, u32[]{:S(2)}, u32[]{:S(2)}) collective-permute-start(bf16[8,2,128,256]{3,2,1,0:T(8,128)(2,1)} %get-tuple-element.40.refs_1_), channel_id=1, source_target_pairs={{48,32},{56,24},{64,80},{80,64},{88,56},{96,112},{112,96},{120,88}... | collective-permute-start | bytes 3145736 | tf_op jit(solution)/shard_map/ppermute | solution.py:245
  49.0 0.7 copy-start.6
  53.6 35.2 %all-to-all-start = ((bf16[8,512,128]{2,1,0:T(8,128)(2,1)}), bf16[8,512,128]{2,1,0:T(8,128)(2,1)S(1)}, u32[]{:S(2)}, u32[]{:S(2)}) async-start(bf16[8,512,128]{2,1,0:T(8,128)(2,1)} %cross.5), calls=%async_computation | async-start | bytes 2097152 | tf_op jit(solution)/shard_map/all_to_all | solution.py:258
  57.7 26.5 %copy-start.4 = (bf16[8,2,128,256]{3,2,1,0:T(8,128)(2,1)S(1)}, bf16[8,2,128,256]{3,2,1,0:T(8,128)(2,1)}, u32[]{:S(2)}) copy-start(bf16[8,2,128,256]{3,2,1,0:T(8,128)(2,1)} %get-tuple-element.40.refs_1_) | copy-start | bytes 3145732
  57.7 26.5 %copy-start.5 = (bf16[8,2,128,256]{3,2,1,0:T(8,128)(2,1)S(1)}, bf16[8,2,128,256]{3,2,1,0:T(8,128)(2,1)}, u32[]{:S(2)}) copy-start(bf16[8,2,128,256]{3,2,1,0:T(8,128)(2,1)} %get-tuple-element.34.refs_4_) | copy-start | bytes 3145732
  63.5 42.2 %collective-permute-start.4 = (bf16[8,2,128,256]{3,2,1,0:T(8,128)(2,1)}, bf16[8,2,128,256]{3,2,1,0:T(8,128)(2,1)}, u32[]{:S(2)}, u32[]{:S(2)}) collective-permute-start(bf16[8,2,128,256]{3,2,1,0:T(8,128)(2,1)} %get-tuple-element.39.refs_1_), channel_id=1, source_target_pairs={{0,40},{8,32},{16,24},{24,80},{32,72},{40,64},{48,56},{56,112},{64... | collective-permute-start | bytes 3145736 | tf_op jit(solution)/shard_map/ppermute | solution.py:248
  82.6 38.8 %collective-permute-start.10 = (bf16[8,2,128,256]{3,2,1,0:T(8,128)(2,1)}, bf16[8,2,128,256]{3,2,1,0:T(8,128)(2,1)}, u32[]{:S(2)}, u32[]{:S(2)}) collective-permute-start(bf16[8,2,128,256]{3,2,1,0:T(8,128)(2,1)} %get-tuple-element.39.refs_1_), channel_id=1, source_target_pairs={{48,32},{56,24},{64,80},{80,64},{88,56},{96,112},{112,96},{120,88}... | collective-permute-start | bytes 3145736 | tf_op jit(solution)/shard_map/ppermute | solution.py:245
  88.7 32.7 %copy-start.3 = (bf16[8,2,128,256]{3,2,1,0:T(8,128)(2,1)S(1)}, bf16[8,2,128,256]{3,2,1,0:T(8,128)(2,1)}, u32[]{:S(2)}) copy-start(bf16[8,2,128,256]{3,2,1,0:T(8,128)(2,1)} %get-tuple-element.39.refs_1_) | copy-start | bytes 3145732
  88.7 35.7 %all-to-all-start.1 = ((bf16[8,512,128]{2,1,0:T(8,128)(2,1)}), bf16[8,512,128]{2,1,0:T(8,128)(2,1)S(1)}, u32[]{:S(2)}, u32[]{:S(2)}) async-start(bf16[8,512,128]{2,1,0:T(8,128)(2,1)} %cross.6), calls=%async_computation.1 | async-start | bytes 2097152 | tf_op jit(solution)/shard_map/all_to_all | solution.py:258
  93.0 36.2 %collective-permute-start.3 = (bf16[8,2,128,256]{3,2,1,0:T(8,128)(2,1)}, bf16[8,2,128,256]{3,2,1,0:T(8,128)(2,1)}, u32[]{:S(2)}, u32[]{:S(2)}) collective-permute-start(bf16[8,2,128,256]{3,2,1,0:T(8,128)(2,1)} %get-tuple-element.37.refs_1_), channel_id=1, source_target_pairs={{0,40},{8,32},{16,24},{24,80},{32,72},{40,64},{48,56},{56,112},{64... | collective-permute-start | bytes 3145736 | tf_op jit(solution)/shard_map/ppermute | solution.py:248
  103.9 25.4 %collective-permute-start.11 = (bf16[8,2,128,256]{3,2,1,0:T(8,128)(2,1)}, bf16[8,2,128,256]{3,2,1,0:T(8,128)(2,1)}, u32[]{:S(2)}, u32[]{:S(2)}) collective-permute-start(bf16[8,2,128,256]{3,2,1,0:T(8,128)(2,1)} %get-tuple-element.37.refs_1_), channel_id=1, source_target_pairs={{48,32},{56,24},{64,80},{80,64},{88,56},{96,112},{112,96},{120,88}... | collective-permute-start | bytes 3145736 | tf_op jit(solution)/shard_map/ppermute | solution.py:245
  105.8 66.0 %collective-permute-start.12 = (bf16[8,2,128,256]{3,2,1,0:T(8,128)(2,1)}, bf16[8,2,128,256]{3,2,1,0:T(8,128)(2,1)}, u32[]{:S(2)}, u32[]{:S(2)}) collective-permute-start(bf16[8,2,128,256]{3,2,1,0:T(8,128)(2,1)} %get-tuple-element.50.refs_2_), channel_id=1, source_target_pairs={{40,0},{48,8},{56,16},{64,24},{72,32},{80,40},{88,48},{96,56},{104... | collective-permute-start | bytes 3145736 | tf_op jit(solution)/shard_map/ppermute | solution.py:251
  124.4 12.9 %all-to-all-start.2 = ((bf16[8,256,128]{2,1,0:T(8,128)(2,1)}), bf16[8,256,128]{2,1,0:T(8,128)(2,1)S(1)}, u32[]{:S(2)}, u32[]{:S(2)}) async-start(bf16[8,256,128]{2,1,0:T(8,128)(2,1)} %cross.7), calls=%async_computation.2 | async-start | bytes 1048576 | tf_op jit(solution)/shard_map/all_to_all | solution.py:258
  150.2 1.0 copy-start.7
  151.2 20.6 %copy-start.2 = (bf16[8,2,128,256]{3,2,1,0:T(8,128)(2,1)S(1)}, bf16[8,2,128,256]{3,2,1,0:T(8,128)(2,1)}, u32[]{:S(2)}) copy-start(bf16[8,2,128,256]{3,2,1,0:T(8,128)(2,1)} %get-tuple-element.48.refs_0_) | copy-start | bytes 3145732
  152.2 36.2 %collective-permute-start.13 = (bf16[2048,256]{1,0:T(8,128)(2,1)S(1)}, bf16[2048,256]{1,0:T(8,128)(2,1)S(1)}, u32[]{:S(2)}, u32[]{:S(2)}) collective-permute-start(bf16[2048,256]{1,0:T(8,128)(2,1)S(1)} %to_lags.3), channel_id=1, source_target_pairs={{40,0},{32,8},{24,16},{80,24},{72,32},{64,40},{56,48},{112,56},{10... | collective-permute-start | bytes 3145736 | tf_op jit(solution)/shard_map/ppermute | solution.py:267

commit v4 on v3

--- a/solution.py
+++ b/solution.py
@@ -30,9 +30,8 @@
     ("send", 7, "p0"),
     ("third", 7, "p0"),
     ("send", 6, "g5"),
-    ("join", (5,), "v1", "p0"),
-    ("join", (7,), "v2", "p1"),
-    ("join", (3, 6), "v3", "p2"),
+    ("join", (5, 7), "v1", "p0"),
+    ("join", (3, 6), "v2", "p1"),
 )
 
 
@@ -105,7 +104,6 @@
         x_ref, y_refs, refs = refs[0], refs[1 : 1 + sources], refs[1 + sources :]
         count, _, channels, windows = x_ref.shape
         depth = 2 * count
-        norm = 1.0 / windows**0.5
         for f in range(count):
             x = x_ref[f].reshape(2 * channels, windows)
             y = y_refs[0][f]
@@ -118,8 +116,8 @@
             low, high = product[:channels], product[channels:]
             real = low[:, :channels] + high[:, channels:]
             imag = high[:, :channels] - low[:, channels:]
-            acc[pl.ds(f, channels, stride=depth), :] = real * norm
-            acc[pl.ds(count + f, channels, stride=depth), :] = imag * norm
+            acc[pl.ds(f, channels, stride=depth), :] = real
+            acc[pl.ds(count + f, channels, stride=depth), :] = imag
         rows = channels * depth // bands
         for band in range(bands):
             part = acc[band * rows : (band + 1) * rows, :]
@@ -206,7 +204,7 @@
     _, freq_local, channels, windows = spectra.shape
     bands = lax.axis_size("band")
     behind, ahead, third, back = routes(lax.axis_size("pair"))
-    norm = 1.0 / float(freq_local * bands) ** 0.5
+    norm = 1.0 / (float(freq_local * bands) ** 0.5 * float(windows) ** 0.5)
     mask = live[None, :]
     pick = (lax.axis_index("pair") % 4 != 1).astype(jnp.int32)[None]
     counts = [eighths * freq_local // 8 for _, eighths in GROUPS]

time: 193 us -> 195 us (1.010)
  waiting for transfers between devices: 25.7 us -> 53.2 us
  starting transfers between devices: 97.9 us -> 71.5 us
  Pallas kernels: 34.2 us -> 31.7 us
  blocking collectives: 25.6 us -> 27.7 us
    ppermute x5, waiting for transfers between devices: 7.66 us -> 38 us  [local(): moved = there[f'g{what}'] = lax.ppermute(sent, 'pair', ahead)]
    ppermute x3, starting transfers between devices: 25 us -> 7.88 us  [local(): moved = there[f'g{what}'] = lax.ppermute(sent, 'pair', behind)]
    ppermute x5, starting transfers between devices: 31.8 us -> 24 us  [local(): moved = there[f'g{what}'] = lax.ppermute(sent, 'pair', ahead)]
    all_to_all x3 -> x2, waiting for transfers between devices: 5.56 us -> 0.01 us  [local(): piece = lax.all_to_all(value, 'band', 0, 0)]
    all_to_all x3 -> x2, starting transfers between devices: 13.2 us -> 9.01 us  [local(): piece = lax.all_to_all(value, 'band', 0, 0)]
    ppermute x3, waiting for transfers between devices: 12.5 us -> 15.2 us  [local(): moved = there[f'g{what}'] = lax.ppermute(sent, 'pair', behind)]
    ppermute x1, starting transfers between devices: 19.5 us -> 22.2 us  [local(): far = lax.ppermute(far, 'pair', back)]
    pallas_call x5 -> x4, Pallas kernels: 16.9 us -> 14.5 us  [cross(): pl.pallas_call(functools.partial(cross_kernel, [len(ys) for _, ys in grou...]
  transfers between devices with their start and end apart: 17 -> 16, of which waited for: 5 -> 5; matrix products, arithmetic and copies ran while one was open for 2% -> 2% of each run, Pallas kernels for 16% -> 14%
where the time goes in v4:
time: 195 us; the launch traced here: 194 us
  starting transfers between devices  71.5 us (37%)
  waiting for transfers between devices  53.2 us (27%)
  Pallas kernels  31.7 us (16%)
  blocking collectives  27.7 us (14%)
  other arithmetic  5.87 us (3%)
  local copies, waits for them, and re-layouts  3.23 us (2%)
    ppermute x5, waiting for transfers between devices, local(): moved = there[f'g{what}'] = lax.ppermute(sent, 'pair', ahead)  38 us
    all_to_all x2, blocking collectives, local(): piece = lax.all_to_all(value, 'band', 0, 0)  27.7 us
    ppermute x5, starting transfers between devices, local(): moved = there[f'g{what}'] = lax.ppermute(sent, 'pair', ahead)  24 us
    ppermute x1, starting transfers between devices, local(): far = lax.ppermute(far, 'pair', back)  22.2 us
    pallas_call x3, Pallas kernels, whiten(): pl.pallas_call(functools.partial(whiten_kernel, starts), grid=(starts[-1]...  15.5 us
    ppermute x3, waiting for transfers between devices, local(): moved = there[f'g{what}'] = lax.ppermute(sent, 'pair', behind)  15.2 us
    pallas_call x4, Pallas kernels, cross(): pl.pallas_call(functools.partial(cross_kernel, [len(ys) for _, ys in grou...  14.5 us
    all_to_all x2, starting transfers between devices, local(): piece = lax.all_to_all(value, 'band', 0, 0)  9.01 us
  transfers between devices with their start and end apart: 16, of which 5 were waited for; matrix products, arithmetic and copies ran while one was open for 2% of the time, Pallas kernels for 14%

profile of v4, /device:TPU:1, one launch (start us, length us, event | category | flops | bytes accessed | tf_op | source)
XLA Modules:
  0.0 193.6 jit_solution(3355002282918709828)
XLA Ops:
  0.0 4.1 %whiten.3 = (bf16[8,2,128,256]{3,2,1,0:T(8,128)(2,1)}, bf16[8,2,128,256]{3,2,1,0:T(8,128)(2,1)}) custom-call(bf16[2,64,128,256]{3,2,1,0:T(8,128)(2,1)} %x_ref.3, s32[1,128]{1,0:T(1,128)} %bitcast.18), custom_call_target="tpu_custom_call" | custom-call | flops 8388608 | bytes 4194304 | tf_op jit(solution)/shard_map/whiten/pallas_call | solution.py:77
  4.1 3.0 %collective-permute-start.1 = (bf16[8,2,128,256]{3,2,1,0:T(8,128)(2,1)}, bf16[8,2,128,256]{3,2,1,0:T(8,128)(2,1)S(1)}, u32[]{:S(2)}, u32[]{:S(2)}) collective-permute-start(bf16[8,2,128,256]{3,2,1,0:T(8,128)(2,1)} %get-tuple-element.29.refs_3_), channel_id=1, source_target_pairs={{0,40},{8,32},{16,24},{24,80},{32,72},{40,64},{48,56},{56,112},{64... | collective-permute-start | bytes 3145736 | tf_op jit(solution)/shard_map/ppermute | solution.py:246
  7.1 1.7 collective-permute-start.2
  8.8 5.7 %whiten.4 = (bf16[8,2,128,256]{3,2,1,0:T(8,128)(2,1)}, bf16[8,2,128,256]{3,2,1,0:T(8,128)(2,1)}, bf16[8,2,128,256]{3,2,1,0:T(8,128)(2,1)}) custom-call(bf16[2,64,128,256]{3,2,1,0:T(8,128)(2,1)} %x_ref.3, s32[1,128]{1,0:T(1,128)} %bitcast.19), custom_call_target="tpu_custom_call" | custom-call | flops 12582912 | bytes 6291456 | tf_op jit(solution)/shard_map/whiten/pallas_call | solution.py:77
  14.6 3.5 %collective-permute-start.7 = (bf16[8,2,128,256]{3,2,1,0:T(8,128)(2,1)}, bf16[8,2,128,256]{3,2,1,0:T(8,128)(2,1)}, u32[]{:S(2)}, u32[]{:S(2)}) collective-permute-start(bf16[8,2,128,256]{3,2,1,0:T(8,128)(2,1)} %get-tuple-element.32.refs_4_), channel_id=1, source_target_pairs={{0,40},{8,32},{16,24},{24,80},{32,72},{40,64},{48,56},{56,112},{64... | collective-permute-start | bytes 3145736 | tf_op jit(solution)/shard_map/ppermute | solution.py:246
  18.1 1.7 collective-permute-start.8
  19.8 4.9 %collective-permute-start = (bf16[8,2,128,256]{3,2,1,0:T(8,128)(2,1)S(1)}, bf16[8,2,128,256]{3,2,1,0:T(8,128)(2,1)}, u32[]{:S(2)}, u32[]{:S(2)}) collective-permute-start(bf16[8,2,128,256]{3,2,1,0:T(8,128)(2,1)S(1)} %copy-done), channel_id=1, source_target_pairs={{40,0},{48,8},{56,16},{64,24},{72,32},{80,40},{88,48},{96,56},{104... | collective-permute-start | bytes 3145736 | tf_op jit(solution)/shard_map/ppermute | solution.py:249
  24.8 0.1 iota_add_fusion
  24.9 0.1 iota_add_fusion.1
  24.9 0.1 iota_add_fusion.2
  25.0 0.1 iota_add_fusion.3
  25.1 0.1 iota_add_fusion.4
  25.2 0.1 iota_add_fusion.5
  25.2 0.1 iota_add_fusion.6
  25.3 0.1 iota_add_fusion.7
  25.4 2.9 %cosine_convert_fusion.2 = (bf16[8,1,8,256]{3,2,1,0:T(8,128)(2,1)S(1)}, bf16[8,1,8,256]{3,2,1,0:T(8,128)(2,1)S(1)}, bf16[8,1,8,256]{3,2,1,0:T(8,128)(2,1)S(1)}, ...) fusion(s32[256]{0:T(256)S(1)} %iota_add_fusion.8, ...), kind=kLoop, calls=%fused_computation.79 | loop fusion | flops 2228224 | bytes 527360 | tf_op jit(solution)/shard_map/convert.5
  28.3 0.8 pad_maximum_fusion.3
  29.2 0.7 copy-done.7
  29.9 5.4 %collective-permute-done.1.refs_2_ = bf16[8,2,128,256]{3,2,1,0:T(8,128)(2,1)S(1)} collective-permute-done((bf16[8,2,128,256]{3,2,1,0:T(8,128)(2,1)}, bf16[8,2,128,256]{3,2,1,0:T(8,128)(2,1)S(1)}, u32[]{:S(2)}, u32[]{:S(2)}) %collective-permute-start.1) | collective-permute-done | bytes 1048608 | tf_op jit(solution)/shard_map/ppermute | solution.py:246
  35.3 0.0 collective-permute-start.4
  35.3 0.0 collective-permute-done.2.refs_4_
  35.3 3.0 %collective-permute-start.5 = (bf16[8,2,128,256]{3,2,1,0:T(8,128)(2,1)}, bf16[8,2,128,256]{3,2,1,0:T(8,128)(2,1)}, u32[]{:S(2)}, u32[]{:S(2)}) collective-permute-start(bf16[8,2,128,256]{3,2,1,0:T(8,128)(2,1)} %get-tuple-element.44.refs_0_), channel_id=1, source_target_pairs={{40,0},{48,8},{56,16},{64,24},{72,32},{80,40},{88,48},{96,56},{104... | collective-permute-start | bytes 3145736 | tf_op jit(solution)/shard_map/ppermute | solution.py:249
  38.3 15.2 %collective-permute-done.refs_1_ = bf16[8,2,128,256]{3,2,1,0:T(8,128)(2,1)} collective-permute-done((bf16[8,2,128,256]{3,2,1,0:T(8,128)(2,1)S(1)}, bf16[8,2,128,256]{3,2,1,0:T(8,128)(2,1)}, u32[]{:S(2)}, u32[]{:S(2)}) %collective-permute-start) | collective-permute-done | bytes 1048608 | tf_op jit(solution)/shard_map/ppermute | solution.py:249
  53.6 3.7 %cross.4 = bf16[8,512,128]{2,1,0:T(8,128)(2,1)} custom-call(s32[1]{0:T(128)} %bitcast.pick_ref, bf16[8,2,128,256]{3,2,1,0:T(8,128)(2,1)S(1)} %copy-done, bf16[8,2,128,256]{3,2,1,0:T(8,128)(2,1)} %collective-permute-done.refs_1_, bf16[8,2,128,256]{3,2,1,0:T(8,128)(2,1)S(1)} %collective-permute-done.1.refs_2_, bf16[8,2,128,256]{3,2,1,0:T(8,128)(2,1)S(1)} %copy-done.1, ...), custom_call_target="tpu_custom_call" | custom-call | flops 536870912 | bytes 5242880 | tf_op jit(solution)/shard_map/cross/pallas_call | solution.py:132
  57.3 5.4 %all-to-all-start = ((bf16[8,512,128]{2,1,0:T(8,128)(2,1)}), bf16[8,512,128]{2,1,0:T(8,128)(2,1)S(1)}, u32[]{:S(2)}, u32[]{:S(2)}) async-start(bf16[8,512,128]{2,1,0:T(8,128)(2,1)} %cross.4), calls=%async_computation | async-start | bytes 2097152 | tf_op jit(solution)/shard_map/all_to_all | solution.py:256
  62.7 1.8 collective-permute-start.6
  64.5 5.7 %whiten.5 = (bf16[8,2,128,256]{3,2,1,0:T(8,128)(2,1)}, bf16[8,2,128,256]{3,2,1,0:T(8,128)(2,1)}, bf16[8,2,128,256]{3,2,1,0:T(8,128)(2,1)}) custom-call(bf16[2,64,128,256]{3,2,1,0:T(8,128)(2,1)} %x_ref.3, s32[1,128]{1,0:T(1,128)} %bitcast.20), custom_call_target="tpu_custom_call" | custom-call | flops 12582912 | bytes 6291456 | tf_op jit(solution)/shard_map/whiten/pallas_call | solution.py:77
  70.2 9.2 %collective-permute-done.4.refs_0_ = bf16[8,2,128,256]{3,2,1,0:T(8,128)(2,1)} collective-permute-done((bf16[8,2,128,256]{3,2,1,0:T(8,128)(2,1)}, bf16[8,2,128,256]{3,2,1,0:T(8,128)(2,1)}, u32[]{:S(2)}, u32[]{:S(2)}) %collective-permute-start.4) | collective-permute-done | bytes 1048608 | tf_op jit(solution)/shard_map/ppermute | solution.py:246
  79.4 13.4 %collective-permute-start.3 = (bf16[8,2,128,256]{3,2,1,0:T(8,128)(2,1)}, bf16[8,2,128,256]{3,2,1,0:T(8,128)(2,1)}, u32[]{:S(2)}, u32[]{:S(2)}) collective-permute-start(bf16[8,2,128,256]{3,2,1,0:T(8,128)(2,1)} %get-tuple-element.35.refs_1_), channel_id=1, source_target_pairs={{0,40},{8,32},{16,24},{24,80},{32,72},{40,64},{48,56},{56,112},{64... | collective-permute-start | bytes 3145736 | tf_op jit(solution)/shard_map/ppermute | solution.py:246
  92.9 0.0 all-to-all-done.refs_0_
  92.9 0.0 collective-permute-done.5.refs_1_
  92.9 1.7 collective-permute-start.9
  94.6 3.9 %collective-permute-start.10 = (bf16[8,2,128,256]{3,2,1,0:T(8,128)(2,1)}, bf16[8,2,128,256]{3,2,1,0:T(8,128)(2,1)}, u32[]{:S(2)}, u32[]{:S(2)}) collective-permute-start(bf16[8,2,128,256]{3,2,1,0:T(8,128)(2,1)} %get-tuple-element.42.refs_4_), channel_id=1, source_target_pairs={{0,40},{8,32},{16,24},{24,80},{32,72},{40,64},{48,56},{56,112},{64... | collective-permute-start | bytes 3145736 | tf_op jit(solution)/shard_map/ppermute | solution.py:246
  98.5 1.6 collective-permute-start.11
  100.2 4.3 %cross.5 = bf16[8,512,128]{2,1,0:T(8,128)(2,1)} custom-call(s32[1]{0:T(128)} %bitcast.pick_ref, bf16[8,2,128,256]{3,2,1,0:T(8,128)(2,1)} %collective-permute-done.4.refs_0_, bf16[8,2,128,256]{3,2,1,0:T(8,128)(2,1)S(1)} %copy-done.3, bf16[8,2,128,256]{3,2,1,0:T(8,128)(2,1)} %collective-permute-done.6.refs_2_, ...), custom_call_target="tpu_custom_call" | custom-call | flops 536870912 | bytes 5242880 | tf_op jit(solution)/shard_map/cross/pallas_call | solution.py:132
  104.5 3.6 %all-to-all-start.1 = ((bf16[8,512,128]{2,1,0:T(8,128)(2,1)}), bf16[8,512,128]{2,1,0:T(8,128)(2,1)S(1)}, u32[]{:S(2)}, u32[]{:S(2)}) async-start(bf16[8,512,128]{2,1,0:T(8,128)(2,1)} %cross.5), calls=%async_computation.1 | async-start | bytes 2097152 | tf_op jit(solution)/shard_map/all_to_all | solution.py:256
  108.1 9.6 %collective-permute-done.3.refs_0_ = bf16[8,2,128,256]{3,2,1,0:T(8,128)(2,1)} collective-permute-done((bf16[8,2,128,256]{3,2,1,0:T(8,128)(2,1)}, bf16[8,2,128,256]{3,2,1,0:T(8,128)(2,1)}, u32[]{:S(2)}, u32[]{:S(2)}) %collective-permute-start.3) | collective-permute-done | bytes 1048608 | tf_op jit(solution)/shard_map/ppermute | solution.py:246
  117.6 13.8 %collective-permute-done.10.refs_3_ = bf16[8,2,128,256]{3,2,1,0:T(8,128)(2,1)} collective-permute-done((bf16[8,2,128,256]{3,2,1,0:T(8,128)(2,1)}, bf16[8,2,128,256]{3,2,1,0:T(8,128)(2,1)}, u32[]{:S(2)}, u32[]{:S(2)}) %collective-permute-start.10) | collective-permute-done | bytes 1048608 | tf_op jit(solution)/shard_map/ppermute | solution.py:246
  131.4 1.2 copy-done.5
  132.7 1.2 copy-done.6
  133.9 3.4 %cross.6 = bf16[8,512,128]{2,1,0:T(8,128)(2,1)S(1)} custom-call(s32[1]{0:T(128)} %bitcast.pick_ref, bf16[8,2,128,256]{3,2,1,0:T(8,128)(2,1)} %collective-permute-done.3.refs_0_, bf16[8,2,128,256]{3,2,1,0:T(8,128)(2,1)S(1)} %copy-done.5, bf16[8,2,128,256]{3,2,1,0:T(8,128)(2,1)} %collective-permute-done.9.refs_2_, ...), custom_call_target="tpu_custom_call" | custom-call | flops 536870912 | bytes 5242880 | tf_op jit(solution)/shard_map/cross/pallas_call | solution.py:132
  137.3 14.9 %all_to_all.20.refs_3_.refs_4_ = bf16[8,512,128]{2,1,0:T(8,128)(2,1)S(1)} all-to-all(bf16[8,512,128]{2,1,0:T(8,128)(2,1)S(1)} %cross.6), channel_id=1, replica_groups=mesh['pair'=32,'band'=8] {'band'}, dimensions={0} | all-to-all | bytes 2097152 | tf_op jit(solution)/shard_map/all_to_all | solution.py:256
  152.2 1.0 to_lags.3
  153.2 22.2 %collective-permute-start.13 = (bf16[2048,256]{1,0:T(8,128)(2,1)S(1)}, bf16[2048,256]{1,0:T(8,128)(2,1)S(1)}, u32[]{:S(2)}, u32[]{:S(2)}) collective-permute-start(bf16[2048,256]{1,0:T(8,128)(2,1)S(1)} %to_lags.3), channel_id=1, source_target_pairs={{40,0},{32,8},{24,16},{80,24},{72,32},{64,40},{56,48},{112,56},{10... | collective-permute-start | bytes 3145736 | tf_op jit(solution)/shard_map/ppermute | solution.py:265
  175.4 3.0 %cross.7 = bf16[8,512,128]{2,1,0:T(8,128)(2,1)S(1)} custom-call(s32[1]{0:T(128)} %bitcast.pick_ref, bf16[8,2,128,256]{3,2,1,0:T(8,128)(2,1)S(1)} %copy-done.2, bf16[8,2,128,256]{3,2,1,0:T(8,128)(2,1)} %collective-permute-done.5.refs_1_, bf16[8,2,128,256]{3,2,1,0:T(8,128)(2,1)} %get-tuple-element.46.refs_2_, ...), custom_call_target="tpu_custom_call" | custom-call | flops 536870912 | bytes 5242880 | tf_op jit(solution)/shard_map/cross/pallas_call | solution.py:132
  178.5 12.8 %all_to_all.21.refs_1_.refs_2_ = bf16[8,512,128]{2,1,0:T(8,128)(2,1)S(1)} all-to-all(bf16[8,512,128]{2,1,0:T(8,128)(2,1)S(1)} %cross.7), channel_id=1, replica_groups=mesh['pair'=32,'band'=8] {'band'}, dimensions={0} | all-to-all | bytes 2097152 | tf_op jit(solution)/shard_map/all_to_all | solution.py:256
  191.3 0.8 to_lags.2
  192.0 1.5 convert_add_fusion
  (42 shorter events, 0.2 us)
Async XLA Ops:
  4.1 15.7 %copy-start = (bf16[8,2,128,256]{3,2,1,0:T(8,128)(2,1)S(1)}, bf16[8,2,128,256]{3,2,1,0:T(8,128)(2,1)}, u32[]{:S(2)}) copy-start(bf16[8,2,128,256]{3,2,1,0:T(8,128)(2,1)} %get-tuple-element.28.refs_0_) | copy-start | bytes 3145732
  4.1 31.3 %collective-permute-start.1 = (bf16[8,2,128,256]{3,2,1,0:T(8,128)(2,1)}, bf16[8,2,128,256]{3,2,1,0:T(8,128)(2,1)S(1)}, u32[]{:S(2)}, u32[]{:S(2)}) collective-permute-start(bf16[8,2,128,256]{3,2,1,0:T(8,128)(2,1)} %get-tuple-element.29.refs_3_), channel_id=1, source_target_pairs={{0,40},{8,32},{16,24},{24,80},{32,72},{40,64},{48,56},{56,112},{64... | collective-permute-start | bytes 3145736 | tf_op jit(solution)/shard_map/ppermute | solution.py:246
  7.1 28.2 %collective-permute-start.2 = (bf16[8,2,128,256]{3,2,1,0:T(8,128)(2,1)}, bf16[8,2,128,256]{3,2,1,0:T(8,128)(2,1)}, u32[]{:S(2)}, u32[]{:S(2)}) collective-permute-start(bf16[8,2,128,256]{3,2,1,0:T(8,128)(2,1)} %get-tuple-element.29.refs_3_), channel_id=1, source_target_pairs={{48,32},{56,24},{64,80},{80,64},{88,56},{96,112},{112,96},{120,88}... | collective-permute-start | bytes 3145736 | tf_op jit(solution)/shard_map/ppermute | solution.py:243
  14.6 39.0 %copy-start.1 = (bf16[8,2,128,256]{3,2,1,0:T(8,128)(2,1)S(1)}, bf16[8,2,128,256]{3,2,1,0:T(8,128)(2,1)}, u32[]{:S(2)}) copy-start(bf16[8,2,128,256]{3,2,1,0:T(8,128)(2,1)} %get-tuple-element.29.refs_3_) | copy-start | bytes 3145732
  14.6 80.0 %collective-permute-start.7 = (bf16[8,2,128,256]{3,2,1,0:T(8,128)(2,1)}, bf16[8,2,128,256]{3,2,1,0:T(8,128)(2,1)}, u32[]{:S(2)}, u32[]{:S(2)}) collective-permute-start(bf16[8,2,128,256]{3,2,1,0:T(8,128)(2,1)} %get-tuple-element.32.refs_4_), channel_id=1, source_target_pairs={{0,40},{8,32},{16,24},{24,80},{32,72},{40,64},{48,56},{56,112},{64... | collective-permute-start | bytes 3145736 | tf_op jit(solution)/shard_map/ppermute | solution.py:246
  18.1 80.4 %collective-permute-start.8 = (bf16[8,2,128,256]{3,2,1,0:T(8,128)(2,1)}, bf16[8,2,128,256]{3,2,1,0:T(8,128)(2,1)}, u32[]{:S(2)}, u32[]{:S(2)}) collective-permute-start(bf16[8,2,128,256]{3,2,1,0:T(8,128)(2,1)} %get-tuple-element.32.refs_4_), channel_id=1, source_target_pairs={{48,32},{56,24},{64,80},{80,64},{88,56},{96,112},{112,96},{120,88}... | collective-permute-start | bytes 3145736 | tf_op jit(solution)/shard_map/ppermute | solution.py:243
  19.8 33.8 %collective-permute-start = (bf16[8,2,128,256]{3,2,1,0:T(8,128)(2,1)S(1)}, bf16[8,2,128,256]{3,2,1,0:T(8,128)(2,1)}, u32[]{:S(2)}, u32[]{:S(2)}) collective-permute-start(bf16[8,2,128,256]{3,2,1,0:T(8,128)(2,1)S(1)} %copy-done), channel_id=1, source_target_pairs={{40,0},{48,8},{56,16},{64,24},{72,32},{80,40},{88,48},{96,56},{104... | collective-permute-start | bytes 3145736 | tf_op jit(solution)/shard_map/ppermute | solution.py:249
  29.2 0.7 copy-start.7
  35.3 44.1 %collective-permute-start.4 = (bf16[8,2,128,256]{3,2,1,0:T(8,128)(2,1)}, bf16[8,2,128,256]{3,2,1,0:T(8,128)(2,1)}, u32[]{:S(2)}, u32[]{:S(2)}) collective-permute-start(bf16[8,2,128,256]{3,2,1,0:T(8,128)(2,1)} %get-tuple-element.36.refs_1_), channel_id=1, source_target_pairs={{0,40},{8,32},{16,24},{24,80},{32,72},{40,64},{48,56},{56,112},{64... | collective-permute-start | bytes 3145736 | tf_op jit(solution)/shard_map/ppermute | solution.py:246
  35.3 57.6 %collective-permute-start.5 = (bf16[8,2,128,256]{3,2,1,0:T(8,128)(2,1)}, bf16[8,2,128,256]{3,2,1,0:T(8,128)(2,1)}, u32[]{:S(2)}, u32[]{:S(2)}) collective-permute-start(bf16[8,2,128,256]{3,2,1,0:T(8,128)(2,1)} %get-tuple-element.44.refs_0_), channel_id=1, source_target_pairs={{40,0},{48,8},{56,16},{64,24},{72,32},{80,40},{88,48},{96,56},{104... | collective-permute-start | bytes 3145736 | tf_op jit(solution)/shard_map/ppermute | solution.py:249
  57.3 5.5 %copy-start.3 = (bf16[8,2,128,256]{3,2,1,0:T(8,128)(2,1)S(1)}, bf16[8,2,128,256]{3,2,1,0:T(8,128)(2,1)}, u32[]{:S(2)}) copy-start(bf16[8,2,128,256]{3,2,1,0:T(8,128)(2,1)} %get-tuple-element.36.refs_1_) | copy-start | bytes 3145732
  57.3 35.6 %all-to-all-start = ((bf16[8,512,128]{2,1,0:T(8,128)(2,1)}), bf16[8,512,128]{2,1,0:T(8,128)(2,1)S(1)}, u32[]{:S(2)}, u32[]{:S(2)}) async-start(bf16[8,512,128]{2,1,0:T(8,128)(2,1)} %cross.4), calls=%async_computation | async-start | bytes 2097152 | tf_op jit(solution)/shard_map/all_to_all | solution.py:256
  62.7 37.4 %copy-start.4 = (bf16[8,2,128,256]{3,2,1,0:T(8,128)(2,1)S(1)}, bf16[8,2,128,256]{3,2,1,0:T(8,128)(2,1)}, u32[]{:S(2)}) copy-start(bf16[8,2,128,256]{3,2,1,0:T(8,128)(2,1)} %get-tuple-element.32.refs_4_) | copy-start | bytes 3145732
  62.7 37.4 %collective-permute-start.6 = (bf16[8,2,128,256]{3,2,1,0:T(8,128)(2,1)S(1)}, bf16[8,2,128,256]{3,2,1,0:T(8,128)(2,1)}, u32[]{:S(2)}, u32[]{:S(2)}) collective-permute-start(bf16[8,2,128,256]{3,2,1,0:T(8,128)(2,1)S(1)} %copy-done.3), channel_id=1, source_target_pairs={{48,32},{56,24},{64,80},{80,64},{88,56},{96,112},{112,96},{120,88}... | collective-permute-start | bytes 3145736 | tf_op jit(solution)/shard_map/ppermute | solution.py:243
  79.4 38.2 %collective-permute-start.3 = (bf16[8,2,128,256]{3,2,1,0:T(8,128)(2,1)}, bf16[8,2,128,256]{3,2,1,0:T(8,128)(2,1)}, u32[]{:S(2)}, u32[]{:S(2)}) collective-permute-start(bf16[8,2,128,256]{3,2,1,0:T(8,128)(2,1)} %get-tuple-element.35.refs_1_), channel_id=1, source_target_pairs={{0,40},{8,32},{16,24},{24,80},{32,72},{40,64},{48,56},{56,112},{64... | collective-permute-start | bytes 3145736 | tf_op jit(solution)/shard_map/ppermute | solution.py:246
  92.9 24.7 %collective-permute-start.9 = (bf16[8,2,128,256]{3,2,1,0:T(8,128)(2,1)}, bf16[8,2,128,256]{3,2,1,0:T(8,128)(2,1)}, u32[]{:S(2)}, u32[]{:S(2)}) collective-permute-start(bf16[8,2,128,256]{3,2,1,0:T(8,128)(2,1)} %get-tuple-element.35.refs_1_), channel_id=1, source_target_pairs={{48,32},{56,24},{64,80},{80,64},{88,56},{96,112},{112,96},{120,88}... | collective-permute-start | bytes 3145736 | tf_op jit(solution)/shard_map/ppermute | solution.py:243
  94.6 36.9 %collective-permute-start.10 = (bf16[8,2,128,256]{3,2,1,0:T(8,128)(2,1)}, bf16[8,2,128,256]{3,2,1,0:T(8,128)(2,1)}, u32[]{:S(2)}, u32[]{:S(2)}) collective-permute-start(bf16[8,2,128,256]{3,2,1,0:T(8,128)(2,1)} %get-tuple-element.42.refs_4_), channel_id=1, source_target_pairs={{0,40},{8,32},{16,24},{24,80},{32,72},{40,64},{48,56},{56,112},{64... | collective-permute-start | bytes 3145736 | tf_op jit(solution)/shard_map/ppermute | solution.py:246
  98.5 32.9 %collective-permute-start.11 = (bf16[8,2,128,256]{3,2,1,0:T(8,128)(2,1)}, bf16[8,2,128,256]{3,2,1,0:T(8,128)(2,1)}, u32[]{:S(2)}, u32[]{:S(2)}) collective-permute-start(bf16[8,2,128,256]{3,2,1,0:T(8,128)(2,1)} %get-tuple-element.42.refs_4_), channel_id=1, source_target_pairs={{48,32},{56,24},{64,80},{80,64},{88,56},{96,112},{112,96},{120,88}... | collective-permute-start | bytes 3145736 | tf_op jit(solution)/shard_map/ppermute | solution.py:243
  104.5 32.8 %all-to-all-start.1 = ((bf16[8,512,128]{2,1,0:T(8,128)(2,1)}), bf16[8,512,128]{2,1,0:T(8,128)(2,1)S(1)}, u32[]{:S(2)}, u32[]{:S(2)}) async-start(bf16[8,512,128]{2,1,0:T(8,128)(2,1)} %cross.5), calls=%async_computation.1 | async-start | bytes 2097152 | tf_op jit(solution)/shard_map/all_to_all | solution.py:256
  117.6 57.8 %collective-permute-start.12 = (bf16[8,2,128,256]{3,2,1,0:T(8,128)(2,1)}, bf16[8,2,128,256]{3,2,1,0:T(8,128)(2,1)}, u32[]{:S(2)}, u32[]{:S(2)}) collective-permute-start(bf16[8,2,128,256]{3,2,1,0:T(8,128)(2,1)} %get-tuple-element.46.refs_2_), channel_id=1, source_target_pairs={{40,0},{48,8},{56,16},{64,24},{72,32},{80,40},{88,48},{96,56},{104... | collective-permute-start | bytes 3145736 | tf_op jit(solution)/shard_map/ppermute | solution.py:249
  131.4 1.2 copy-start.5
  132.7 1.2 copy-start.6
  137.3 14.9 %copy-start.8 = (bf16[640,256]{1,0:T(8,128)(2,1)S(1)}, bf16[640,256]{1,0:T(8,128)(2,1)}, u32[]{:S(2)}) copy-start(bf16[640,256]{1,0:T(8,128)(2,1)} %copy-done.7) | copy-start | bytes 983044
  152.2 23.2 %copy-start.2 = (bf16[8,2,128,256]{3,2,1,0:T(8,128)(2,1)S(1)}, bf16[8,2,128,256]{3,2,1,0:T(8,128)(2,1)}, u32[]{:S(2)}) copy-start(bf16[8,2,128,256]{3,2,1,0:T(8,128)(2,1)} %get-tuple-element.44.refs_0_) | copy-start | bytes 3145732
  153.2 38.8 %collective-permute-start.13 = (bf16[2048,256]{1,0:T(8,128)(2,1)S(1)}, bf16[2048,256]{1,0:T(8,128)(2,1)S(1)}, u32[]{:S(2)}, u32[]{:S(2)}) collective-permute-start(bf16[2048,256]{1,0:T(8,128)(2,1)S(1)} %to_lags.3), channel_id=1, source_target_pairs={{40,0},{32,8},{24,16},{80,24},{72,32},{64,40},{56,48},{112,56},{10... | collective-permute-start | bytes 3145736 | tf_op jit(solution)/shard_map/ppermute | solution.py:265
